TPU v7x, 32 devices: a whole 2x2x4 slice. The times are simulated.
32 devices in a mesh: parts: 2 (over x), blk: 16 (over z, y, core).
Axes of the slice: x: 2, y: 2, z: 4, core: 2. Of those that a mesh axis runs over, the one named last changes fastest.
Arguments:
- queries: bfloat16 [256, 4096], P(('parts', 'blk')), parts along dimension 0, may hold values from -48 to 48
- key_cache: bfloat16 [8192, 512], P(('parts', 'blk')), parts along dimension 0, may hold values from -6 to 6
- value_cache: bfloat16 [8192, 512], P(('parts', 'blk')), parts along dimension 0, may hold values from -6 to 6
- tile_page: int32 [8192], P(('parts', 'blk')), parts along dimension 0, may hold values from 0 to 15, never falling along the last dimension, each value on 1 to 512 neighbouring positions
- row_last: int32 [256], P(('parts', 'blk')), parts along dimension 0, may hold values from 0 to 15, as said below
Outputs:
- attention_out: bfloat16 [256, 4096], P(('parts', 'blk')), parts along dimension 0
There are 2 independent parts, one for each index of `parts`. A program takes and returns all parts, laid end to end along the dimension named above; each array names one. Nothing has to cross between parts.
Inputs may be any that keep to these rules, and one draw needn't show every extreme that they name: tile_page never falls along the tile tokens; every page of 0 to 15 has between 1 and 512 tokens, one exactly 512. row_last never falls along the text rows; the first row sees page 0 only and the last row sees every page.
All inputs are finite; a program needn't handle non-finite values.
Results may differ from a plain program's by a relative error of at most 0.00575.
Values may be sent and summed in bfloat16 or wider, within the bound.
A program may use at most 64 MiB of HBM per device.

v0:
```python
import math

import jax
import jax.numpy as jnp
from jax import lax
from jax.sharding import PartitionSpec as P

HEADS = 32
KV_HEADS = 4
HEAD_DIM = 128


NEGATIVE_FILL = -1e30


def shifted(block, axis, distance):
    devices = range(lax.axis_size(axis))
    route = [((i - distance) % len(devices), i) for i in devices]
    return lax.ppermute(block, axis, route)


def absorb_block(queries, carried, key_cache, value_cache, tile_page):
    run_max, run_sum, last_float, run_out = carried
    row_count = queries.shape[0]
    group_size = HEADS // KV_HEADS
    q_heads = queries.reshape(row_count, KV_HEADS, group_size, HEAD_DIM)
    k_heads = key_cache.reshape(key_cache.shape[0], KV_HEADS, HEAD_DIM)
    v_heads = value_cache.reshape(value_cache.shape[0], KV_HEADS, HEAD_DIM)
    scores = jnp.einsum("rkgd,tkd->rkgt", q_heads, k_heads, preferred_element_type=jnp.float32)
    scores = scores * (1.0 / math.sqrt(HEAD_DIM))
    last_page = last_float.astype(jnp.int32)
    visible = (tile_page[None, :] <= last_page[:, None])[:, None, None, :]
    masked = jnp.where(visible, scores, NEGATIVE_FILL)
    new_max = jnp.maximum(run_max, jnp.max(masked, axis=-1))
    weights = jnp.where(visible, jnp.exp(scores - new_max[..., None]), 0.0)
    factor = jnp.exp(run_max - new_max)
    new_sum = run_sum * factor + jnp.sum(weights, axis=-1)
    update = jnp.einsum(
        "rkgt,tkd->rkgd", weights.astype(jnp.bfloat16), v_heads, preferred_element_type=jnp.float32
    )
    new_out = run_out * factor[..., None] + update
    return (new_max, new_sum, last_float, new_out)


def visit_block(queries, carried, key_cache, value_cache, tile_page):
    return absorb_block(queries, carried, key_cache, value_cache, tile_page)


def fresh_state(last_rows):
    row_count = last_rows.shape[0]
    group_size = HEADS // KV_HEADS
    run_max = jnp.full((row_count, KV_HEADS, group_size), NEGATIVE_FILL, jnp.float32)
    run_sum = jnp.zeros((row_count, KV_HEADS, group_size), jnp.float32)
    run_out = jnp.zeros((row_count, KV_HEADS, group_size, HEAD_DIM), jnp.float32)
    return (run_max, run_sum, last_rows.astype(jnp.float32), run_out)


def finish(carried):
    run_sum = carried[1]
    run_out = carried[3]
    result = (run_out / run_sum[..., None]).astype(jnp.bfloat16)
    return result.reshape(run_out.shape[0], HEADS * HEAD_DIM)


def shards(queries, key_cache, value_cache, tile_page, row_last):
    blocks = lax.axis_size("blk")
    half_rows = queries.shape[0] // 2
    front_rows = queries[:half_rows]
    rear_rows = queries[half_rows:]
    front_last = row_last[:half_rows]
    rear_last = row_last[half_rows:]
    own_rows = jnp.concatenate([front_rows, rear_rows], axis=0)
    own_last = jnp.concatenate([front_last, rear_last], axis=0)
    carried = visit_block(own_rows, fresh_state(own_last), key_cache, value_cache, tile_page)

    def turn(turn_index, carry_pair):
        query_rows, state_tuple = carry_pair
        query_rows = shifted(query_rows, "blk", 1)
        state_tuple = shifted(
            (state_tuple[0], state_tuple[1], state_tuple[2], state_tuple[3]), "blk", 1
        )
        return (query_rows, visit_block(query_rows, state_tuple, key_cache, value_cache, tile_page))

    final_pair = lax.fori_loop(0, blocks - 1, turn, (own_rows, carried))
    done_rows = shifted(finish(final_pair[1]), "blk", 1)
    front_done = done_rows[:half_rows]
    rear_done = done_rows[half_rows:]
    return jnp.concatenate([front_done, rear_done], axis=0)


def solution(mesh):
    placed = (
        P(("parts", "blk"), None),
        P(("parts", "blk"), None),
        P(("parts", "blk"), None),
        P(("parts", "blk")),
        P(("parts", "blk")),
    )
    return jax.shard_map(
        shards, mesh=mesh, in_specs=placed, out_specs=P(("parts", "blk"), None), check_vma=False
    )
```

profile of v0, /device:TPU:0, one launch (start us, length us, event | category | flops | bytes accessed | tf_op | source)
XLA Modules:
  0.0 150.0 jit_solution(10820893675862077489)
XLA Ops:
  0.0 0.8 copy.90
  0.8 1.1 reshape.77
  2.0 0.9 copy-done.1
  5.2 137.7 %while.19 = (s32[]{:T(128)}, bf16[8,4096]{1,0:T(8,128)(2,1)S(1)}, f32[8,4,8]{2,0,1:T(8,128)S(1)}, f32[8,4,8]{2,0,1:T(8,128)S(1)}, f32[8]{0:T(128)S(1)}, /*index=...) while((s32[]{:T(128)}, bf16[8,4096]{1,0:T(8,128)(2,1)S(1)}, ...), condition=%wide.wide.region_5.6_spmd, body=%wide.wide.region_2.5_spmd.sunk | while | flops 34212360 | bytes 2588253 | solution.py:84
  5.7 2.6 %collective-permute-start = (bf16[8,4096]{1,0:T(8,128)(2,1)S(1)}, bf16[8,4096]{1,0:T(8,128)(2,1)S(1)}, u32[]{:S(2)}, u32[]{:S(2)}) collective-permute-start(bf16[8,4096]{1,0:T(8,128)(2,1)S(1)} %get-tuple-element.210), channel_id=1, source_target_pairs={{15,0},{0,1},{1,2},{2,3},{3,4},{4,5},{5,6},{6,7},{7,8},{8,9},{9,10... | collective-permute-start | bytes 196616 | tf_op jit(solution)/shard_map/while/body/eval_jaxpr/ppermute | solution.py:19
  8.4 1.6 %collective-permute-start.3 = (f32[8,4,8]{2,0,1:T(8,128)S(1)}, f32[8,4,8]{2,0,1:T(8,128)S(1)}, u32[]{:S(2)}, u32[]{:S(2)}) collective-permute-start(f32[8,4,8]{2,0,1:T(8,128)S(1)} %get-tuple-element.212), channel_id=1, source_target_pairs={{15,0},{0,1},{1,2},{2,3},{3,4},{4,5},{5,6},{6,7},{7,8},{8,9},{9,10... | collective-permute-start | bytes 3080 | tf_op jit(solution)/shard_map/while/body/eval_jaxpr/ppermute | solution.py:19
  10.0 1.9 %collective-permute-done.2 = f32[8]{0:T(128)S(1)} collective-permute-done((f32[8]{0:T(128)S(1)}, f32[8]{0:T(128)S(1)}, u32[]{:S(2)}, u32[]{:S(2)}) %collective-permute-start.2) | collective-permute-done | bytes 64 | tf_op jit(solution)/shard_map/while/body/eval_jaxpr/ppermute | solution.py:19
  12.0 0.7 collective-permute-done
  13.0 1.2 collective-permute-done.1
  14.4 2.6 %collective-permute-done.4 = f32[8,4,8,128]{3,2,0,1:T(8,128)S(1)} collective-permute-done((f32[8,4,8,128]{3,2,0,1:T(8,128)S(1)}, f32[8,4,8,128]{3,2,0,1:T(8,128)S(1)}, u32[]{:S(2)}, u32[]{:S(2)}) %collective-permute-start.4) | collective-permute-done | bytes 131104 | tf_op jit(solution)/shard_map/while/body/eval_jaxpr/ppermute | solution.py:19
  17.5 1.3 collective-permute-start.3
  18.9 4.1 %collective-permute-done.2 = f32[8]{0:T(128)S(1)} collective-permute-done((f32[8]{0:T(128)S(1)}, f32[8]{0:T(128)S(1)}, u32[]{:S(2)}, u32[]{:S(2)}) %collective-permute-start.2) | collective-permute-done | bytes 64 | tf_op jit(solution)/shard_map/while/body/eval_jaxpr/ppermute | solution.py:19
  23.1 0.7 collective-permute-done
  24.4 1.5 %collective-permute-done.4 = f32[8,4,8,128]{3,2,0,1:T(8,128)S(1)} collective-permute-done((f32[8,4,8,128]{3,2,0,1:T(8,128)S(1)}, f32[8,4,8,128]{3,2,0,1:T(8,128)S(1)}, u32[]{:S(2)}, u32[]{:S(2)}) %collective-permute-start.4) | collective-permute-done | bytes 131104 | tf_op jit(solution)/shard_map/while/body/eval_jaxpr/ppermute | solution.py:19
  26.4 1.3 collective-permute-start.3
  27.8 4.1 %collective-permute-done.2 = f32[8]{0:T(128)S(1)} collective-permute-done((f32[8]{0:T(128)S(1)}, f32[8]{0:T(128)S(1)}, u32[]{:S(2)}, u32[]{:S(2)}) %collective-permute-start.2) | collective-permute-done | bytes 64 | tf_op jit(solution)/shard_map/while/body/eval_jaxpr/ppermute | solution.py:19
  32.0 0.7 collective-permute-done
  33.2 1.5 %collective-permute-done.4 = f32[8,4,8,128]{3,2,0,1:T(8,128)S(1)} collective-permute-done((f32[8,4,8,128]{3,2,0,1:T(8,128)S(1)}, f32[8,4,8,128]{3,2,0,1:T(8,128)S(1)}, u32[]{:S(2)}, u32[]{:S(2)}) %collective-permute-start.4) | collective-permute-done | bytes 131104 | tf_op jit(solution)/shard_map/while/body/eval_jaxpr/ppermute | solution.py:19
  35.4 5.4 %collective-permute-done.2 = f32[8]{0:T(128)S(1)} collective-permute-done((f32[8]{0:T(128)S(1)}, f32[8]{0:T(128)S(1)}, u32[]{:S(2)}, u32[]{:S(2)}) %collective-permute-start.2) | collective-permute-done | bytes 64 | tf_op jit(solution)/shard_map/while/body/eval_jaxpr/ppermute | solution.py:19
  40.8 0.7 collective-permute-done
  42.1 1.2 collective-permute-done.4
  43.8 2.1 %collective-permute-start.3 = (f32[8,4,8]{2,0,1:T(8,128)S(1)}, f32[8,4,8]{2,0,1:T(8,128)S(1)}, u32[]{:S(2)}, u32[]{:S(2)}) collective-permute-start(f32[8,4,8]{2,0,1:T(8,128)S(1)} %get-tuple-element.212), channel_id=1, source_target_pairs={{15,0},{0,1},{1,2},{2,3},{3,4},{4,5},{5,6},{6,7},{7,8},{8,9},{9,10... | collective-permute-start | bytes 3080 | tf_op jit(solution)/shard_map/while/body/eval_jaxpr/ppermute | solution.py:19
  45.9 3.3 %collective-permute-done.2 = f32[8]{0:T(128)S(1)} collective-permute-done((f32[8]{0:T(128)S(1)}, f32[8]{0:T(128)S(1)}, u32[]{:S(2)}, u32[]{:S(2)}) %collective-permute-start.2) | collective-permute-done | bytes 64 | tf_op jit(solution)/shard_map/while/body/eval_jaxpr/ppermute | solution.py:19
  50.6 2.3 %collective-permute-done.4 = f32[8,4,8,128]{3,2,0,1:T(8,128)S(1)} collective-permute-done((f32[8,4,8,128]{3,2,0,1:T(8,128)S(1)}, f32[8,4,8,128]{3,2,0,1:T(8,128)S(1)}, u32[]{:S(2)}, u32[]{:S(2)}) %collective-permute-start.4) | collective-permute-done | bytes 131104 | tf_op jit(solution)/shard_map/while/body/eval_jaxpr/ppermute | solution.py:19
  53.4 1.3 collective-permute-start.3
  54.8 4.1 %collective-permute-done.2 = f32[8]{0:T(128)S(1)} collective-permute-done((f32[8]{0:T(128)S(1)}, f32[8]{0:T(128)S(1)}, u32[]{:S(2)}, u32[]{:S(2)}) %collective-permute-start.2) | collective-permute-done | bytes 64 | tf_op jit(solution)/shard_map/while/body/eval_jaxpr/ppermute | solution.py:19
  59.0 0.7 collective-permute-done
  60.3 1.5 %collective-permute-done.4 = f32[8,4,8,128]{3,2,0,1:T(8,128)S(1)} collective-permute-done((f32[8,4,8,128]{3,2,0,1:T(8,128)S(1)}, f32[8,4,8,128]{3,2,0,1:T(8,128)S(1)}, u32[]{:S(2)}, u32[]{:S(2)}) %collective-permute-start.4) | collective-permute-done | bytes 131104 | tf_op jit(solution)/shard_map/while/body/eval_jaxpr/ppermute | solution.py:19
  62.3 1.3 collective-permute-start.3
  63.7 4.1 %collective-permute-done.2 = f32[8]{0:T(128)S(1)} collective-permute-done((f32[8]{0:T(128)S(1)}, f32[8]{0:T(128)S(1)}, u32[]{:S(2)}, u32[]{:S(2)}) %collective-permute-start.2) | collective-permute-done | bytes 64 | tf_op jit(solution)/shard_map/while/body/eval_jaxpr/ppermute | solution.py:19
  67.9 0.7 collective-permute-done
  69.2 1.5 %collective-permute-done.4 = f32[8,4,8,128]{3,2,0,1:T(8,128)S(1)} collective-permute-done((f32[8,4,8,128]{3,2,0,1:T(8,128)S(1)}, f32[8,4,8,128]{3,2,0,1:T(8,128)S(1)}, u32[]{:S(2)}, u32[]{:S(2)}) %collective-permute-start.4) | collective-permute-done | bytes 131104 | tf_op jit(solution)/shard_map/while/body/eval_jaxpr/ppermute | solution.py:19
  71.2 1.0 collective-permute-start.3
  72.2 4.5 %collective-permute-done.2 = f32[8]{0:T(128)S(1)} collective-permute-done((f32[8]{0:T(128)S(1)}, f32[8]{0:T(128)S(1)}, u32[]{:S(2)}, u32[]{:S(2)}) %collective-permute-start.2) | collective-permute-done | bytes 64 | tf_op jit(solution)/shard_map/while/body/eval_jaxpr/ppermute | solution.py:19
  76.8 0.7 collective-permute-done
  78.1 1.2 collective-permute-done.4
  79.7 2.1 %collective-permute-start.3 = (f32[8,4,8]{2,0,1:T(8,128)S(1)}, f32[8,4,8]{2,0,1:T(8,128)S(1)}, u32[]{:S(2)}, u32[]{:S(2)}) collective-permute-start(f32[8,4,8]{2,0,1:T(8,128)S(1)} %get-tuple-element.212), channel_id=1, source_target_pairs={{15,0},{0,1},{1,2},{2,3},{3,4},{4,5},{5,6},{6,7},{7,8},{8,9},{9,10... | collective-permute-start | bytes 3080 | tf_op jit(solution)/shard_map/while/body/eval_jaxpr/ppermute | solution.py:19
  81.9 3.3 %collective-permute-done.2 = f32[8]{0:T(128)S(1)} collective-permute-done((f32[8]{0:T(128)S(1)}, f32[8]{0:T(128)S(1)}, u32[]{:S(2)}, u32[]{:S(2)}) %collective-permute-start.2) | collective-permute-done | bytes 64 | tf_op jit(solution)/shard_map/while/body/eval_jaxpr/ppermute | solution.py:19
  86.6 2.3 %collective-permute-done.4 = f32[8,4,8,128]{3,2,0,1:T(8,128)S(1)} collective-permute-done((f32[8,4,8,128]{3,2,0,1:T(8,128)S(1)}, f32[8,4,8,128]{3,2,0,1:T(8,128)S(1)}, u32[]{:S(2)}, u32[]{:S(2)}) %collective-permute-start.4) | collective-permute-done | bytes 131104 | tf_op jit(solution)/shard_map/while/body/eval_jaxpr/ppermute | solution.py:19
  89.4 1.3 collective-permute-start.3
  90.8 4.1 %collective-permute-done.2 = f32[8]{0:T(128)S(1)} collective-permute-done((f32[8]{0:T(128)S(1)}, f32[8]{0:T(128)S(1)}, u32[]{:S(2)}, u32[]{:S(2)}) %collective-permute-start.2) | collective-permute-done | bytes 64 | tf_op jit(solution)/shard_map/while/body/eval_jaxpr/ppermute | solution.py:19
  95.0 0.7 collective-permute-done
  96.2 1.5 %collective-permute-done.4 = f32[8,4,8,128]{3,2,0,1:T(8,128)S(1)} collective-permute-done((f32[8,4,8,128]{3,2,0,1:T(8,128)S(1)}, f32[8,4,8,128]{3,2,0,1:T(8,128)S(1)}, u32[]{:S(2)}, u32[]{:S(2)}) %collective-permute-start.4) | collective-permute-done | bytes 131104 | tf_op jit(solution)/shard_map/while/body/eval_jaxpr/ppermute | solution.py:19
  98.2 1.3 collective-permute-start.3
  99.6 4.1 %collective-permute-done.2 = f32[8]{0:T(128)S(1)} collective-permute-done((f32[8]{0:T(128)S(1)}, f32[8]{0:T(128)S(1)}, u32[]{:S(2)}, u32[]{:S(2)}) %collective-permute-start.2) | collective-permute-done | bytes 64 | tf_op jit(solution)/shard_map/while/body/eval_jaxpr/ppermute | solution.py:19
  103.8 0.7 collective-permute-done
  105.1 1.5 %collective-permute-done.4 = f32[8,4,8,128]{3,2,0,1:T(8,128)S(1)} collective-permute-done((f32[8,4,8,128]{3,2,0,1:T(8,128)S(1)}, f32[8,4,8,128]{3,2,0,1:T(8,128)S(1)}, u32[]{:S(2)}, u32[]{:S(2)}) %collective-permute-start.4) | collective-permute-done | bytes 131104 | tf_op jit(solution)/shard_map/while/body/eval_jaxpr/ppermute | solution.py:19
  107.1 1.0 collective-permute-start.3
  108.1 4.5 %collective-permute-done.2 = f32[8]{0:T(128)S(1)} collective-permute-done((f32[8]{0:T(128)S(1)}, f32[8]{0:T(128)S(1)}, u32[]{:S(2)}, u32[]{:S(2)}) %collective-permute-start.2) | collective-permute-done | bytes 64 | tf_op jit(solution)/shard_map/while/body/eval_jaxpr/ppermute | solution.py:19
  112.7 0.7 collective-permute-done
  114.0 1.2 collective-permute-done.4
  115.6 2.1 %collective-permute-start.3 = (f32[8,4,8]{2,0,1:T(8,128)S(1)}, f32[8,4,8]{2,0,1:T(8,128)S(1)}, u32[]{:S(2)}, u32[]{:S(2)}) collective-permute-start(f32[8,4,8]{2,0,1:T(8,128)S(1)} %get-tuple-element.212), channel_id=1, source_target_pairs={{15,0},{0,1},{1,2},{2,3},{3,4},{4,5},{5,6},{6,7},{7,8},{8,9},{9,10... | collective-permute-start | bytes 3080 | tf_op jit(solution)/shard_map/while/body/eval_jaxpr/ppermute | solution.py:19
  117.8 3.3 %collective-permute-done.2 = f32[8]{0:T(128)S(1)} collective-permute-done((f32[8]{0:T(128)S(1)}, f32[8]{0:T(128)S(1)}, u32[]{:S(2)}, u32[]{:S(2)}) %collective-permute-start.2) | collective-permute-done | bytes 64 | tf_op jit(solution)/shard_map/while/body/eval_jaxpr/ppermute | solution.py:19
  121.2 0.7 collective-permute-done
  122.5 2.3 %collective-permute-done.4 = f32[8,4,8,128]{3,2,0,1:T(8,128)S(1)} collective-permute-done((f32[8,4,8,128]{3,2,0,1:T(8,128)S(1)}, f32[8,4,8,128]{3,2,0,1:T(8,128)S(1)}, u32[]{:S(2)}, u32[]{:S(2)}) %collective-permute-start.4) | collective-permute-done | bytes 131104 | tf_op jit(solution)/shard_map/while/body/eval_jaxpr/ppermute | solution.py:19
  125.3 1.3 collective-permute-start.3
  126.7 4.1 %collective-permute-done.2 = f32[8]{0:T(128)S(1)} collective-permute-done((f32[8]{0:T(128)S(1)}, f32[8]{0:T(128)S(1)}, u32[]{:S(2)}, u32[]{:S(2)}) %collective-permute-start.2) | collective-permute-done | bytes 64 | tf_op jit(solution)/shard_map/while/body/eval_jaxpr/ppermute | solution.py:19
  130.9 0.7 collective-permute-done
  132.2 1.5 %collective-permute-done.4 = f32[8,4,8,128]{3,2,0,1:T(8,128)S(1)} collective-permute-done((f32[8,4,8,128]{3,2,0,1:T(8,128)S(1)}, f32[8,4,8,128]{3,2,0,1:T(8,128)S(1)}, u32[]{:S(2)}, u32[]{:S(2)}) %collective-permute-start.4) | collective-permute-done | bytes 131104 | tf_op jit(solution)/shard_map/while/body/eval_jaxpr/ppermute | solution.py:19
  134.2 1.3 collective-permute-start.3
  135.6 4.1 %collective-permute-done.2 = f32[8]{0:T(128)S(1)} collective-permute-done((f32[8]{0:T(128)S(1)}, f32[8]{0:T(128)S(1)}, u32[]{:S(2)}, u32[]{:S(2)}) %collective-permute-start.2) | collective-permute-done | bytes 64 | tf_op jit(solution)/shard_map/while/body/eval_jaxpr/ppermute | solution.py:19
  139.8 0.7 collective-permute-done
  141.0 1.5 %collective-permute-done.4 = f32[8,4,8,128]{3,2,0,1:T(8,128)S(1)} collective-permute-done((f32[8,4,8,128]{3,2,0,1:T(8,128)S(1)}, f32[8,4,8,128]{3,2,0,1:T(8,128)S(1)}, u32[]{:S(2)}, u32[]{:S(2)}) %collective-permute-start.4) | collective-permute-done | bytes 131104 | tf_op jit(solution)/shard_map/while/body/eval_jaxpr/ppermute | solution.py:19
  143.0 6.4 %collective-permute-done.5 = bf16[8,4096]{1,0:T(8,128)(2,1)S(1)} collective-permute-done((bf16[8,4096]{1,0:T(8,128)(2,1)S(1)}, bf16[8,4096]{1,0:T(8,128)(2,1)S(1)}, u32[]{:S(2)}, u32[]{:S(2)}) %collective-permute-start.5) | collective-permute-done | bytes 65568 | tf_op jit(solution)/shard_map/ppermute | solution.py:19
  (247 shorter events, 21.1 us)
Async XLA Ops:
  5.2 6.7 %collective-permute-start.2 = (f32[8]{0:T(128)S(1)}, f32[8]{0:T(128)S(1)}, u32[]{:S(2)}, u32[]{:S(2)}) collective-permute-start(f32[8]{0:T(128)S(1)} %get-tuple-element.213), channel_id=1, source_target_pairs={{15,0},{0,1},{1,2},{2,3},{3,4},{4,5},{5,6},{6,7},{7,8},{8,9},{9,10... | collective-permute-start | bytes 104 | tf_op jit(solution)/shard_map/while/body/eval_jaxpr/ppermute | solution.py:19
  5.7 7.0 %collective-permute-start = (bf16[8,4096]{1,0:T(8,128)(2,1)S(1)}, bf16[8,4096]{1,0:T(8,128)(2,1)S(1)}, u32[]{:S(2)}, u32[]{:S(2)}) collective-permute-start(bf16[8,4096]{1,0:T(8,128)(2,1)S(1)} %get-tuple-element.210), channel_id=1, source_target_pairs={{15,0},{0,1},{1,2},{2,3},{3,4},{4,5},{5,6},{6,7},{7,8},{8,9},{9,10... | collective-permute-start | bytes 196616 | tf_op jit(solution)/shard_map/while/body/eval_jaxpr/ppermute | solution.py:19
  8.3 5.9 %collective-permute-start.1 = (f32[8,4,8]{2,0,1:T(8,128)S(1)}, f32[8,4,8]{2,0,1:T(8,128)S(1)}, u32[]{:S(2)}, u32[]{:S(2)}) collective-permute-start(f32[8,4,8]{2,0,1:T(8,128)S(1)} %get-tuple-element.211), channel_id=1, source_target_pairs={{15,0},{0,1},{1,2},{2,3},{3,4},{4,5},{5,6},{6,7},{7,8},{8,9},{9,10... | collective-permute-start | bytes 3080 | tf_op jit(solution)/shard_map/while/body/eval_jaxpr/ppermute | solution.py:19
  8.4 6.0 %collective-permute-start.3 = (f32[8,4,8]{2,0,1:T(8,128)S(1)}, f32[8,4,8]{2,0,1:T(8,128)S(1)}, u32[]{:S(2)}, u32[]{:S(2)}) collective-permute-start(f32[8,4,8]{2,0,1:T(8,128)S(1)} %get-tuple-element.212), channel_id=1, source_target_pairs={{15,0},{0,1},{1,2},{2,3},{3,4},{4,5},{5,6},{6,7},{7,8},{8,9},{9,10... | collective-permute-start | bytes 3080 | tf_op jit(solution)/shard_map/while/body/eval_jaxpr/ppermute | solution.py:19
  9.9 7.1 %collective-permute-start.4 = (f32[8,4,8,128]{3,2,0,1:T(8,128)S(1)}, f32[8,4,8,128]{3,2,0,1:T(8,128)S(1)}, u32[]{:S(2)}, u32[]{:S(2)}) collective-permute-start(f32[8,4,8,128]{3,2,0,1:T(8,128)S(1)} %get-tuple-element.214), channel_id=1, source_target_pairs={{15,0},{0,1},{1,2},{2,3},{3,4},{4,5},{5,6},{6,7},{7,8},{8,9},{9,10... | collective-permute-start | bytes 393224 | tf_op jit(solution)/shard_map/while/body/eval_jaxpr/ppermute | solution.py:19
  17.3 5.7 %collective-permute-start.2 = (f32[8]{0:T(128)S(1)}, f32[8]{0:T(128)S(1)}, u32[]{:S(2)}, u32[]{:S(2)}) collective-permute-start(f32[8]{0:T(128)S(1)} %get-tuple-element.213), channel_id=1, source_target_pairs={{15,0},{0,1},{1,2},{2,3},{3,4},{4,5},{5,6},{6,7},{7,8},{8,9},{9,10... | collective-permute-start | bytes 104 | tf_op jit(solution)/shard_map/while/body/eval_jaxpr/ppermute | solution.py:19
  17.4 6.4 %collective-permute-start = (bf16[8,4096]{1,0:T(8,128)(2,1)S(1)}, bf16[8,4096]{1,0:T(8,128)(2,1)S(1)}, u32[]{:S(2)}, u32[]{:S(2)}) collective-permute-start(bf16[8,4096]{1,0:T(8,128)(2,1)S(1)} %get-tuple-element.210), channel_id=1, source_target_pairs={{15,0},{0,1},{1,2},{2,3},{3,4},{4,5},{5,6},{6,7},{7,8},{8,9},{9,10... | collective-permute-start | bytes 196616 | tf_op jit(solution)/shard_map/while/body/eval_jaxpr/ppermute | solution.py:19
  17.4 6.7 %collective-permute-start.1 = (f32[8,4,8]{2,0,1:T(8,128)S(1)}, f32[8,4,8]{2,0,1:T(8,128)S(1)}, u32[]{:S(2)}, u32[]{:S(2)}) collective-permute-start(f32[8,4,8]{2,0,1:T(8,128)S(1)} %get-tuple-element.211), channel_id=1, source_target_pairs={{15,0},{0,1},{1,2},{2,3},{3,4},{4,5},{5,6},{6,7},{7,8},{8,9},{9,10... | collective-permute-start | bytes 3080 | tf_op jit(solution)/shard_map/while/body/eval_jaxpr/ppermute | solution.py:19
  17.5 6.9 %collective-permute-start.3 = (f32[8,4,8]{2,0,1:T(8,128)S(1)}, f32[8,4,8]{2,0,1:T(8,128)S(1)}, u32[]{:S(2)}, u32[]{:S(2)}) collective-permute-start(f32[8,4,8]{2,0,1:T(8,128)S(1)} %get-tuple-element.212), channel_id=1, source_target_pairs={{15,0},{0,1},{1,2},{2,3},{3,4},{4,5},{5,6},{6,7},{7,8},{8,9},{9,10... | collective-permute-start | bytes 3080 | tf_op jit(solution)/shard_map/while/body/eval_jaxpr/ppermute | solution.py:19
  18.8 7.1 %collective-permute-start.4 = (f32[8,4,8,128]{3,2,0,1:T(8,128)S(1)}, f32[8,4,8,128]{3,2,0,1:T(8,128)S(1)}, u32[]{:S(2)}, u32[]{:S(2)}) collective-permute-start(f32[8,4,8,128]{3,2,0,1:T(8,128)S(1)} %get-tuple-element.214), channel_id=1, source_target_pairs={{15,0},{0,1},{1,2},{2,3},{3,4},{4,5},{5,6},{6,7},{7,8},{8,9},{9,10... | collective-permute-start | bytes 393224 | tf_op jit(solution)/shard_map/while/body/eval_jaxpr/ppermute | solution.py:19
  26.2 5.7 %collective-permute-start.2 = (f32[8]{0:T(128)S(1)}, f32[8]{0:T(128)S(1)}, u32[]{:S(2)}, u32[]{:S(2)}) collective-permute-start(f32[8]{0:T(128)S(1)} %get-tuple-element.213), channel_id=1, source_target_pairs={{15,0},{0,1},{1,2},{2,3},{3,4},{4,5},{5,6},{6,7},{7,8},{8,9},{9,10... | collective-permute-start | bytes 104 | tf_op jit(solution)/shard_map/while/body/eval_jaxpr/ppermute | solution.py:19
  26.2 6.4 %collective-permute-start = (bf16[8,4096]{1,0:T(8,128)(2,1)S(1)}, bf16[8,4096]{1,0:T(8,128)(2,1)S(1)}, u32[]{:S(2)}, u32[]{:S(2)}) collective-permute-start(bf16[8,4096]{1,0:T(8,128)(2,1)S(1)} %get-tuple-element.210), channel_id=1, source_target_pairs={{15,0},{0,1},{1,2},{2,3},{3,4},{4,5},{5,6},{6,7},{7,8},{8,9},{9,10... | collective-permute-start | bytes 196616 | tf_op jit(solution)/shard_map/while/body/eval_jaxpr/ppermute | solution.py:19
  26.3 6.7 %collective-permute-start.1 = (f32[8,4,8]{2,0,1:T(8,128)S(1)}, f32[8,4,8]{2,0,1:T(8,128)S(1)}, u32[]{:S(2)}, u32[]{:S(2)}) collective-permute-start(f32[8,4,8]{2,0,1:T(8,128)S(1)} %get-tuple-element.211), channel_id=1, source_target_pairs={{15,0},{0,1},{1,2},{2,3},{3,4},{4,5},{5,6},{6,7},{7,8},{8,9},{9,10... | collective-permute-start | bytes 3080 | tf_op jit(solution)/shard_map/while/body/eval_jaxpr/ppermute | solution.py:19
  26.4 6.9 %collective-permute-start.3 = (f32[8,4,8]{2,0,1:T(8,128)S(1)}, f32[8,4,8]{2,0,1:T(8,128)S(1)}, u32[]{:S(2)}, u32[]{:S(2)}) collective-permute-start(f32[8,4,8]{2,0,1:T(8,128)S(1)} %get-tuple-element.212), channel_id=1, source_target_pairs={{15,0},{0,1},{1,2},{2,3},{3,4},{4,5},{5,6},{6,7},{7,8},{8,9},{9,10... | collective-permute-start | bytes 3080 | tf_op jit(solution)/shard_map/while/body/eval_jaxpr/ppermute | solution.py:19
  27.7 7.1 %collective-permute-start.4 = (f32[8,4,8,128]{3,2,0,1:T(8,128)S(1)}, f32[8,4,8,128]{3,2,0,1:T(8,128)S(1)}, u32[]{:S(2)}, u32[]{:S(2)}) collective-permute-start(f32[8,4,8,128]{3,2,0,1:T(8,128)S(1)} %get-tuple-element.214), channel_id=1, source_target_pairs={{15,0},{0,1},{1,2},{2,3},{3,4},{4,5},{5,6},{6,7},{7,8},{8,9},{9,10... | collective-permute-start | bytes 393224 | tf_op jit(solution)/shard_map/while/body/eval_jaxpr/ppermute | solution.py:19
  35.1 6.4 %collective-permute-start = (bf16[8,4096]{1,0:T(8,128)(2,1)S(1)}, bf16[8,4096]{1,0:T(8,128)(2,1)S(1)}, u32[]{:S(2)}, u32[]{:S(2)}) collective-permute-start(bf16[8,4096]{1,0:T(8,128)(2,1)S(1)} %get-tuple-element.210), channel_id=1, source_target_pairs={{15,0},{0,1},{1,2},{2,3},{3,4},{4,5},{5,6},{6,7},{7,8},{8,9},{9,10... | collective-permute-start | bytes 196616 | tf_op jit(solution)/shard_map/while/body/eval_jaxpr/ppermute | solution.py:19
  35.2 6.7 %collective-permute-start.1 = (f32[8,4,8]{2,0,1:T(8,128)S(1)}, f32[8,4,8]{2,0,1:T(8,128)S(1)}, u32[]{:S(2)}, u32[]{:S(2)}) collective-permute-start(f32[8,4,8]{2,0,1:T(8,128)S(1)} %get-tuple-element.211), channel_id=1, source_target_pairs={{15,0},{0,1},{1,2},{2,3},{3,4},{4,5},{5,6},{6,7},{7,8},{8,9},{9,10... | collective-permute-start | bytes 3080 | tf_op jit(solution)/shard_map/while/body/eval_jaxpr/ppermute | solution.py:19
  35.2 6.9 %collective-permute-start.3 = (f32[8,4,8]{2,0,1:T(8,128)S(1)}, f32[8,4,8]{2,0,1:T(8,128)S(1)}, u32[]{:S(2)}, u32[]{:S(2)}) collective-permute-start(f32[8,4,8]{2,0,1:T(8,128)S(1)} %get-tuple-element.212), channel_id=1, source_target_pairs={{15,0},{0,1},{1,2},{2,3},{3,4},{4,5},{5,6},{6,7},{7,8},{8,9},{9,10... | collective-permute-start | bytes 3080 | tf_op jit(solution)/shard_map/while/body/eval_jaxpr/ppermute | solution.py:19
  35.3 8.0 %collective-permute-start.4 = (f32[8,4,8,128]{3,2,0,1:T(8,128)S(1)}, f32[8,4,8,128]{3,2,0,1:T(8,128)S(1)}, u32[]{:S(2)}, u32[]{:S(2)}) collective-permute-start(f32[8,4,8,128]{3,2,0,1:T(8,128)S(1)} %get-tuple-element.214), channel_id=1, source_target_pairs={{15,0},{0,1},{1,2},{2,3},{3,4},{4,5},{5,6},{6,7},{7,8},{8,9},{9,10... | collective-permute-start | bytes 393224 | tf_op jit(solution)/shard_map/while/body/eval_jaxpr/ppermute | solution.py:19
  43.6 6.4 %collective-permute-start = (bf16[8,4096]{1,0:T(8,128)(2,1)S(1)}, bf16[8,4096]{1,0:T(8,128)(2,1)S(1)}, u32[]{:S(2)}, u32[]{:S(2)}) collective-permute-start(bf16[8,4096]{1,0:T(8,128)(2,1)S(1)} %get-tuple-element.210), channel_id=1, source_target_pairs={{15,0},{0,1},{1,2},{2,3},{3,4},{4,5},{5,6},{6,7},{7,8},{8,9},{9,10... | collective-permute-start | bytes 196616 | tf_op jit(solution)/shard_map/while/body/eval_jaxpr/ppermute | solution.py:19
  43.7 6.7 %collective-permute-start.1 = (f32[8,4,8]{2,0,1:T(8,128)S(1)}, f32[8,4,8]{2,0,1:T(8,128)S(1)}, u32[]{:S(2)}, u32[]{:S(2)}) collective-permute-start(f32[8,4,8]{2,0,1:T(8,128)S(1)} %get-tuple-element.211), channel_id=1, source_target_pairs={{15,0},{0,1},{1,2},{2,3},{3,4},{4,5},{5,6},{6,7},{7,8},{8,9},{9,10... | collective-permute-start | bytes 3080 | tf_op jit(solution)/shard_map/while/body/eval_jaxpr/ppermute | solution.py:19
  43.8 6.9 %collective-permute-start.3 = (f32[8,4,8]{2,0,1:T(8,128)S(1)}, f32[8,4,8]{2,0,1:T(8,128)S(1)}, u32[]{:S(2)}, u32[]{:S(2)}) collective-permute-start(f32[8,4,8]{2,0,1:T(8,128)S(1)} %get-tuple-element.212), channel_id=1, source_target_pairs={{15,0},{0,1},{1,2},{2,3},{3,4},{4,5},{5,6},{6,7},{7,8},{8,9},{9,10... | collective-permute-start | bytes 3080 | tf_op jit(solution)/shard_map/while/body/eval_jaxpr/ppermute | solution.py:19
  45.9 7.1 %collective-permute-start.4 = (f32[8,4,8,128]{3,2,0,1:T(8,128)S(1)}, f32[8,4,8,128]{3,2,0,1:T(8,128)S(1)}, u32[]{:S(2)}, u32[]{:S(2)}) collective-permute-start(f32[8,4,8,128]{3,2,0,1:T(8,128)S(1)} %get-tuple-element.214), channel_id=1, source_target_pairs={{15,0},{0,1},{1,2},{2,3},{3,4},{4,5},{5,6},{6,7},{7,8},{8,9},{9,10... | collective-permute-start | bytes 393224 | tf_op jit(solution)/shard_map/while/body/eval_jaxpr/ppermute | solution.py:19
  53.3 6.4 %collective-permute-start = (bf16[8,4096]{1,0:T(8,128)(2,1)S(1)}, bf16[8,4096]{1,0:T(8,128)(2,1)S(1)}, u32[]{:S(2)}, u32[]{:S(2)}) collective-permute-start(bf16[8,4096]{1,0:T(8,128)(2,1)S(1)} %get-tuple-element.210), channel_id=1, source_target_pairs={{15,0},{0,1},{1,2},{2,3},{3,4},{4,5},{5,6},{6,7},{7,8},{8,9},{9,10... | collective-permute-start | bytes 196616 | tf_op jit(solution)/shard_map/while/body/eval_jaxpr/ppermute | solution.py:19
  53.4 6.7 %collective-permute-start.1 = (f32[8,4,8]{2,0,1:T(8,128)S(1)}, f32[8,4,8]{2,0,1:T(8,128)S(1)}, u32[]{:S(2)}, u32[]{:S(2)}) collective-permute-start(f32[8,4,8]{2,0,1:T(8,128)S(1)} %get-tuple-element.211), channel_id=1, source_target_pairs={{15,0},{0,1},{1,2},{2,3},{3,4},{4,5},{5,6},{6,7},{7,8},{8,9},{9,10... | collective-permute-start | bytes 3080 | tf_op jit(solution)/shard_map/while/body/eval_jaxpr/ppermute | solution.py:19
  53.4 6.9 %collective-permute-start.3 = (f32[8,4,8]{2,0,1:T(8,128)S(1)}, f32[8,4,8]{2,0,1:T(8,128)S(1)}, u32[]{:S(2)}, u32[]{:S(2)}) collective-permute-start(f32[8,4,8]{2,0,1:T(8,128)S(1)} %get-tuple-element.212), channel_id=1, source_target_pairs={{15,0},{0,1},{1,2},{2,3},{3,4},{4,5},{5,6},{6,7},{7,8},{8,9},{9,10... | collective-permute-start | bytes 3080 | tf_op jit(solution)/shard_map/while/body/eval_jaxpr/ppermute | solution.py:19
  54.8 7.1 %collective-permute-start.4 = (f32[8,4,8,128]{3,2,0,1:T(8,128)S(1)}, f32[8,4,8,128]{3,2,0,1:T(8,128)S(1)}, u32[]{:S(2)}, u32[]{:S(2)}) collective-permute-start(f32[8,4,8,128]{3,2,0,1:T(8,128)S(1)} %get-tuple-element.214), channel_id=1, source_target_pairs={{15,0},{0,1},{1,2},{2,3},{3,4},{4,5},{5,6},{6,7},{7,8},{8,9},{9,10... | collective-permute-start | bytes 393224 | tf_op jit(solution)/shard_map/while/body/eval_jaxpr/ppermute | solution.py:19
  62.2 6.4 %collective-permute-start = (bf16[8,4096]{1,0:T(8,128)(2,1)S(1)}, bf16[8,4096]{1,0:T(8,128)(2,1)S(1)}, u32[]{:S(2)}, u32[]{:S(2)}) collective-permute-start(bf16[8,4096]{1,0:T(8,128)(2,1)S(1)} %get-tuple-element.210), channel_id=1, source_target_pairs={{15,0},{0,1},{1,2},{2,3},{3,4},{4,5},{5,6},{6,7},{7,8},{8,9},{9,10... | collective-permute-start | bytes 196616 | tf_op jit(solution)/shard_map/while/body/eval_jaxpr/ppermute | solution.py:19
  62.2 6.7 %collective-permute-start.1 = (f32[8,4,8]{2,0,1:T(8,128)S(1)}, f32[8,4,8]{2,0,1:T(8,128)S(1)}, u32[]{:S(2)}, u32[]{:S(2)}) collective-permute-start(f32[8,4,8]{2,0,1:T(8,128)S(1)} %get-tuple-element.211), channel_id=1, source_target_pairs={{15,0},{0,1},{1,2},{2,3},{3,4},{4,5},{5,6},{6,7},{7,8},{8,9},{9,10... | collective-permute-start | bytes 3080 | tf_op jit(solution)/shard_map/while/body/eval_jaxpr/ppermute | solution.py:19
  62.3 6.9 %collective-permute-start.3 = (f32[8,4,8]{2,0,1:T(8,128)S(1)}, f32[8,4,8]{2,0,1:T(8,128)S(1)}, u32[]{:S(2)}, u32[]{:S(2)}) collective-permute-start(f32[8,4,8]{2,0,1:T(8,128)S(1)} %get-tuple-element.212), channel_id=1, source_target_pairs={{15,0},{0,1},{1,2},{2,3},{3,4},{4,5},{5,6},{6,7},{7,8},{8,9},{9,10... | collective-permute-start | bytes 3080 | tf_op jit(solution)/shard_map/while/body/eval_jaxpr/ppermute | solution.py:19
  63.6 7.1 %collective-permute-start.4 = (f32[8,4,8,128]{3,2,0,1:T(8,128)S(1)}, f32[8,4,8,128]{3,2,0,1:T(8,128)S(1)}, u32[]{:S(2)}, u32[]{:S(2)}) collective-permute-start(f32[8,4,8,128]{3,2,0,1:T(8,128)S(1)} %get-tuple-element.214), channel_id=1, source_target_pairs={{15,0},{0,1},{1,2},{2,3},{3,4},{4,5},{5,6},{6,7},{7,8},{8,9},{9,10... | collective-permute-start | bytes 393224 | tf_op jit(solution)/shard_map/while/body/eval_jaxpr/ppermute | solution.py:19
  71.0 6.4 %collective-permute-start = (bf16[8,4096]{1,0:T(8,128)(2,1)S(1)}, bf16[8,4096]{1,0:T(8,128)(2,1)S(1)}, u32[]{:S(2)}, u32[]{:S(2)}) collective-permute-start(bf16[8,4096]{1,0:T(8,128)(2,1)S(1)} %get-tuple-element.210), channel_id=1, source_target_pairs={{15,0},{0,1},{1,2},{2,3},{3,4},{4,5},{5,6},{6,7},{7,8},{8,9},{9,10... | collective-permute-start | bytes 196616 | tf_op jit(solution)/shard_map/while/body/eval_jaxpr/ppermute | solution.py:19
  71.1 6.7 %collective-permute-start.1 = (f32[8,4,8]{2,0,1:T(8,128)S(1)}, f32[8,4,8]{2,0,1:T(8,128)S(1)}, u32[]{:S(2)}, u32[]{:S(2)}) collective-permute-start(f32[8,4,8]{2,0,1:T(8,128)S(1)} %get-tuple-element.211), channel_id=1, source_target_pairs={{15,0},{0,1},{1,2},{2,3},{3,4},{4,5},{5,6},{6,7},{7,8},{8,9},{9,10... | collective-permute-start | bytes 3080 | tf_op jit(solution)/shard_map/while/body/eval_jaxpr/ppermute | solution.py:19
  71.2 6.9 %collective-permute-start.3 = (f32[8,4,8]{2,0,1:T(8,128)S(1)}, f32[8,4,8]{2,0,1:T(8,128)S(1)}, u32[]{:S(2)}, u32[]{:S(2)}) collective-permute-start(f32[8,4,8]{2,0,1:T(8,128)S(1)} %get-tuple-element.212), channel_id=1, source_target_pairs={{15,0},{0,1},{1,2},{2,3},{3,4},{4,5},{5,6},{6,7},{7,8},{8,9},{9,10... | collective-permute-start | bytes 3080 | tf_op jit(solution)/shard_map/while/body/eval_jaxpr/ppermute | solution.py:19
  72.1 7.1 %collective-permute-start.4 = (f32[8,4,8,128]{3,2,0,1:T(8,128)S(1)}, f32[8,4,8,128]{3,2,0,1:T(8,128)S(1)}, u32[]{:S(2)}, u32[]{:S(2)}) collective-permute-start(f32[8,4,8,128]{3,2,0,1:T(8,128)S(1)} %get-tuple-element.214), channel_id=1, source_target_pairs={{15,0},{0,1},{1,2},{2,3},{3,4},{4,5},{5,6},{6,7},{7,8},{8,9},{9,10... | collective-permute-start | bytes 393224 | tf_op jit(solution)/shard_map/while/body/eval_jaxpr/ppermute | solution.py:19
  79.6 6.4 %collective-permute-start = (bf16[8,4096]{1,0:T(8,128)(2,1)S(1)}, bf16[8,4096]{1,0:T(8,128)(2,1)S(1)}, u32[]{:S(2)}, u32[]{:S(2)}) collective-permute-start(bf16[8,4096]{1,0:T(8,128)(2,1)S(1)} %get-tuple-element.210), channel_id=1, source_target_pairs={{15,0},{0,1},{1,2},{2,3},{3,4},{4,5},{5,6},{6,7},{7,8},{8,9},{9,10... | collective-permute-start | bytes 196616 | tf_op jit(solution)/shard_map/while/body/eval_jaxpr/ppermute | solution.py:19
  79.6 6.7 %collective-permute-start.1 = (f32[8,4,8]{2,0,1:T(8,128)S(1)}, f32[8,4,8]{2,0,1:T(8,128)S(1)}, u32[]{:S(2)}, u32[]{:S(2)}) collective-permute-start(f32[8,4,8]{2,0,1:T(8,128)S(1)} %get-tuple-element.211), channel_id=1, source_target_pairs={{15,0},{0,1},{1,2},{2,3},{3,4},{4,5},{5,6},{6,7},{7,8},{8,9},{9,10... | collective-permute-start | bytes 3080 | tf_op jit(solution)/shard_map/while/body/eval_jaxpr/ppermute | solution.py:19
  79.7 6.9 %collective-permute-start.3 = (f32[8,4,8]{2,0,1:T(8,128)S(1)}, f32[8,4,8]{2,0,1:T(8,128)S(1)}, u32[]{:S(2)}, u32[]{:S(2)}) collective-permute-start(f32[8,4,8]{2,0,1:T(8,128)S(1)} %get-tuple-element.212), channel_id=1, source_target_pairs={{15,0},{0,1},{1,2},{2,3},{3,4},{4,5},{5,6},{6,7},{7,8},{8,9},{9,10... | collective-permute-start | bytes 3080 | tf_op jit(solution)/shard_map/while/body/eval_jaxpr/ppermute | solution.py:19
  81.8 7.1 %collective-permute-start.4 = (f32[8,4,8,128]{3,2,0,1:T(8,128)S(1)}, f32[8,4,8,128]{3,2,0,1:T(8,128)S(1)}, u32[]{:S(2)}, u32[]{:S(2)}) collective-permute-start(f32[8,4,8,128]{3,2,0,1:T(8,128)S(1)} %get-tuple-element.214), channel_id=1, source_target_pairs={{15,0},{0,1},{1,2},{2,3},{3,4},{4,5},{5,6},{6,7},{7,8},{8,9},{9,10... | collective-permute-start | bytes 393224 | tf_op jit(solution)/shard_map/while/body/eval_jaxpr/ppermute | solution.py:19
  89.2 6.4 %collective-permute-start = (bf16[8,4096]{1,0:T(8,128)(2,1)S(1)}, bf16[8,4096]{1,0:T(8,128)(2,1)S(1)}, u32[]{:S(2)}, u32[]{:S(2)}) collective-permute-start(bf16[8,4096]{1,0:T(8,128)(2,1)S(1)} %get-tuple-element.210), channel_id=1, source_target_pairs={{15,0},{0,1},{1,2},{2,3},{3,4},{4,5},{5,6},{6,7},{7,8},{8,9},{9,10... | collective-permute-start | bytes 196616 | tf_op jit(solution)/shard_map/while/body/eval_jaxpr/ppermute | solution.py:19
  89.3 6.7 %collective-permute-start.1 = (f32[8,4,8]{2,0,1:T(8,128)S(1)}, f32[8,4,8]{2,0,1:T(8,128)S(1)}, u32[]{:S(2)}, u32[]{:S(2)}) collective-permute-start(f32[8,4,8]{2,0,1:T(8,128)S(1)} %get-tuple-element.211), channel_id=1, source_target_pairs={{15,0},{0,1},{1,2},{2,3},{3,4},{4,5},{5,6},{6,7},{7,8},{8,9},{9,10... | collective-permute-start | bytes 3080 | tf_op jit(solution)/shard_map/while/body/eval_jaxpr/ppermute | solution.py:19
  89.4 6.9 %collective-permute-start.3 = (f32[8,4,8]{2,0,1:T(8,128)S(1)}, f32[8,4,8]{2,0,1:T(8,128)S(1)}, u32[]{:S(2)}, u32[]{:S(2)}) collective-permute-start(f32[8,4,8]{2,0,1:T(8,128)S(1)} %get-tuple-element.212), channel_id=1, source_target_pairs={{15,0},{0,1},{1,2},{2,3},{3,4},{4,5},{5,6},{6,7},{7,8},{8,9},{9,10... | collective-permute-start | bytes 3080 | tf_op jit(solution)/shard_map/while/body/eval_jaxpr/ppermute | solution.py:19
  90.7 7.1 %collective-permute-start.4 = (f32[8,4,8,128]{3,2,0,1:T(8,128)S(1)}, f32[8,4,8,128]{3,2,0,1:T(8,128)S(1)}, u32[]{:S(2)}, u32[]{:S(2)}) collective-permute-start(f32[8,4,8,128]{3,2,0,1:T(8,128)S(1)} %get-tuple-element.214), channel_id=1, source_target_pairs={{15,0},{0,1},{1,2},{2,3},{3,4},{4,5},{5,6},{6,7},{7,8},{8,9},{9,10... | collective-permute-start | bytes 393224 | tf_op jit(solution)/shard_map/while/body/eval_jaxpr/ppermute | solution.py:19
  98.1 6.4 %collective-permute-start = (bf16[8,4096]{1,0:T(8,128)(2,1)S(1)}, bf16[8,4096]{1,0:T(8,128)(2,1)S(1)}, u32[]{:S(2)}, u32[]{:S(2)}) collective-permute-start(bf16[8,4096]{1,0:T(8,128)(2,1)S(1)} %get-tuple-element.210), channel_id=1, source_target_pairs={{15,0},{0,1},{1,2},{2,3},{3,4},{4,5},{5,6},{6,7},{7,8},{8,9},{9,10... | collective-permute-start | bytes 196616 | tf_op jit(solution)/shard_map/while/body/eval_jaxpr/ppermute | solution.py:19
  98.2 6.7 %collective-permute-start.1 = (f32[8,4,8]{2,0,1:T(8,128)S(1)}, f32[8,4,8]{2,0,1:T(8,128)S(1)}, u32[]{:S(2)}, u32[]{:S(2)}) collective-permute-start(f32[8,4,8]{2,0,1:T(8,128)S(1)} %get-tuple-element.211), channel_id=1, source_target_pairs={{15,0},{0,1},{1,2},{2,3},{3,4},{4,5},{5,6},{6,7},{7,8},{8,9},{9,10... | collective-permute-start | bytes 3080 | tf_op jit(solution)/shard_map/while/body/eval_jaxpr/ppermute | solution.py:19
  98.2 6.9 %collective-permute-start.3 = (f32[8,4,8]{2,0,1:T(8,128)S(1)}, f32[8,4,8]{2,0,1:T(8,128)S(1)}, u32[]{:S(2)}, u32[]{:S(2)}) collective-permute-start(f32[8,4,8]{2,0,1:T(8,128)S(1)} %get-tuple-element.212), channel_id=1, source_target_pairs={{15,0},{0,1},{1,2},{2,3},{3,4},{4,5},{5,6},{6,7},{7,8},{8,9},{9,10... | collective-permute-start | bytes 3080 | tf_op jit(solution)/shard_map/while/body/eval_jaxpr/ppermute | solution.py:19
  99.6 7.1 %collective-permute-start.4 = (f32[8,4,8,128]{3,2,0,1:T(8,128)S(1)}, f32[8,4,8,128]{3,2,0,1:T(8,128)S(1)}, u32[]{:S(2)}, u32[]{:S(2)}) collective-permute-start(f32[8,4,8,128]{3,2,0,1:T(8,128)S(1)} %get-tuple-element.214), channel_id=1, source_target_pairs={{15,0},{0,1},{1,2},{2,3},{3,4},{4,5},{5,6},{6,7},{7,8},{8,9},{9,10... | collective-permute-start | bytes 393224 | tf_op jit(solution)/shard_map/while/body/eval_jaxpr/ppermute | solution.py:19
  107.0 6.4 %collective-permute-start = (bf16[8,4096]{1,0:T(8,128)(2,1)S(1)}, bf16[8,4096]{1,0:T(8,128)(2,1)S(1)}, u32[]{:S(2)}, u32[]{:S(2)}) collective-permute-start(bf16[8,4096]{1,0:T(8,128)(2,1)S(1)} %get-tuple-element.210), channel_id=1, source_target_pairs={{15,0},{0,1},{1,2},{2,3},{3,4},{4,5},{5,6},{6,7},{7,8},{8,9},{9,10... | collective-permute-start | bytes 196616 | tf_op jit(solution)/shard_map/while/body/eval_jaxpr/ppermute | solution.py:19
  107.0 6.7 %collective-permute-start.1 = (f32[8,4,8]{2,0,1:T(8,128)S(1)}, f32[8,4,8]{2,0,1:T(8,128)S(1)}, u32[]{:S(2)}, u32[]{:S(2)}) collective-permute-start(f32[8,4,8]{2,0,1:T(8,128)S(1)} %get-tuple-element.211), channel_id=1, source_target_pairs={{15,0},{0,1},{1,2},{2,3},{3,4},{4,5},{5,6},{6,7},{7,8},{8,9},{9,10... | collective-permute-start | bytes 3080 | tf_op jit(solution)/shard_map/while/body/eval_jaxpr/ppermute | solution.py:19
  107.1 6.9 %collective-permute-start.3 = (f32[8,4,8]{2,0,1:T(8,128)S(1)}, f32[8,4,8]{2,0,1:T(8,128)S(1)}, u32[]{:S(2)}, u32[]{:S(2)}) collective-permute-start(f32[8,4,8]{2,0,1:T(8,128)S(1)} %get-tuple-element.212), channel_id=1, source_target_pairs={{15,0},{0,1},{1,2},{2,3},{3,4},{4,5},{5,6},{6,7},{7,8},{8,9},{9,10... | collective-permute-start | bytes 3080 | tf_op jit(solution)/shard_map/while/body/eval_jaxpr/ppermute | solution.py:19
  108.1 7.1 %collective-permute-start.4 = (f32[8,4,8,128]{3,2,0,1:T(8,128)S(1)}, f32[8,4,8,128]{3,2,0,1:T(8,128)S(1)}, u32[]{:S(2)}, u32[]{:S(2)}) collective-permute-start(f32[8,4,8,128]{3,2,0,1:T(8,128)S(1)} %get-tuple-element.214), channel_id=1, source_target_pairs={{15,0},{0,1},{1,2},{2,3},{3,4},{4,5},{5,6},{6,7},{7,8},{8,9},{9,10... | collective-permute-start | bytes 393224 | tf_op jit(solution)/shard_map/while/body/eval_jaxpr/ppermute | solution.py:19
  115.5 6.4 %collective-permute-start = (bf16[8,4096]{1,0:T(8,128)(2,1)S(1)}, bf16[8,4096]{1,0:T(8,128)(2,1)S(1)}, u32[]{:S(2)}, u32[]{:S(2)}) collective-permute-start(bf16[8,4096]{1,0:T(8,128)(2,1)S(1)} %get-tuple-element.210), channel_id=1, source_target_pairs={{15,0},{0,1},{1,2},{2,3},{3,4},{4,5},{5,6},{6,7},{7,8},{8,9},{9,10... | collective-permute-start | bytes 196616 | tf_op jit(solution)/shard_map/while/body/eval_jaxpr/ppermute | solution.py:19
  115.6 6.7 %collective-permute-start.1 = (f32[8,4,8]{2,0,1:T(8,128)S(1)}, f32[8,4,8]{2,0,1:T(8,128)S(1)}, u32[]{:S(2)}, u32[]{:S(2)}) collective-permute-start(f32[8,4,8]{2,0,1:T(8,128)S(1)} %get-tuple-element.211), channel_id=1, source_target_pairs={{15,0},{0,1},{1,2},{2,3},{3,4},{4,5},{5,6},{6,7},{7,8},{8,9},{9,10... | collective-permute-start | bytes 3080 | tf_op jit(solution)/shard_map/while/body/eval_jaxpr/ppermute | solution.py:19
  115.6 6.9 %collective-permute-start.3 = (f32[8,4,8]{2,0,1:T(8,128)S(1)}, f32[8,4,8]{2,0,1:T(8,128)S(1)}, u32[]{:S(2)}, u32[]{:S(2)}) collective-permute-start(f32[8,4,8]{2,0,1:T(8,128)S(1)} %get-tuple-element.212), channel_id=1, source_target_pairs={{15,0},{0,1},{1,2},{2,3},{3,4},{4,5},{5,6},{6,7},{7,8},{8,9},{9,10... | collective-permute-start | bytes 3080 | tf_op jit(solution)/shard_map/while/body/eval_jaxpr/ppermute | solution.py:19
  117.7 7.1 %collective-permute-start.4 = (f32[8,4,8,128]{3,2,0,1:T(8,128)S(1)}, f32[8,4,8,128]{3,2,0,1:T(8,128)S(1)}, u32[]{:S(2)}, u32[]{:S(2)}) collective-permute-start(f32[8,4,8,128]{3,2,0,1:T(8,128)S(1)} %get-tuple-element.214), channel_id=1, source_target_pairs={{15,0},{0,1},{1,2},{2,3},{3,4},{4,5},{5,6},{6,7},{7,8},{8,9},{9,10... | collective-permute-start | bytes 393224 | tf_op jit(solution)/shard_map/while/body/eval_jaxpr/ppermute | solution.py:19
  125.2 6.4 %collective-permute-start = (bf16[8,4096]{1,0:T(8,128)(2,1)S(1)}, bf16[8,4096]{1,0:T(8,128)(2,1)S(1)}, u32[]{:S(2)}, u32[]{:S(2)}) collective-permute-start(bf16[8,4096]{1,0:T(8,128)(2,1)S(1)} %get-tuple-element.210), channel_id=1, source_target_pairs={{15,0},{0,1},{1,2},{2,3},{3,4},{4,5},{5,6},{6,7},{7,8},{8,9},{9,10... | collective-permute-start | bytes 196616 | tf_op jit(solution)/shard_map/while/body/eval_jaxpr/ppermute | solution.py:19
  125.2 6.7 %collective-permute-start.1 = (f32[8,4,8]{2,0,1:T(8,128)S(1)}, f32[8,4,8]{2,0,1:T(8,128)S(1)}, u32[]{:S(2)}, u32[]{:S(2)}) collective-permute-start(f32[8,4,8]{2,0,1:T(8,128)S(1)} %get-tuple-element.211), channel_id=1, source_target_pairs={{15,0},{0,1},{1,2},{2,3},{3,4},{4,5},{5,6},{6,7},{7,8},{8,9},{9,10... | collective-permute-start | bytes 3080 | tf_op jit(solution)/shard_map/while/body/eval_jaxpr/ppermute | solution.py:19
  125.3 6.9 %collective-permute-start.3 = (f32[8,4,8]{2,0,1:T(8,128)S(1)}, f32[8,4,8]{2,0,1:T(8,128)S(1)}, u32[]{:S(2)}, u32[]{:S(2)}) collective-permute-start(f32[8,4,8]{2,0,1:T(8,128)S(1)} %get-tuple-element.212), channel_id=1, source_target_pairs={{15,0},{0,1},{1,2},{2,3},{3,4},{4,5},{5,6},{6,7},{7,8},{8,9},{9,10... | collective-permute-start | bytes 3080 | tf_op jit(solution)/shard_map/while/body/eval_jaxpr/ppermute | solution.py:19
  126.6 7.1 %collective-permute-start.4 = (f32[8,4,8,128]{3,2,0,1:T(8,128)S(1)}, f32[8,4,8,128]{3,2,0,1:T(8,128)S(1)}, u32[]{:S(2)}, u32[]{:S(2)}) collective-permute-start(f32[8,4,8,128]{3,2,0,1:T(8,128)S(1)} %get-tuple-element.214), channel_id=1, source_target_pairs={{15,0},{0,1},{1,2},{2,3},{3,4},{4,5},{5,6},{6,7},{7,8},{8,9},{9,10... | collective-permute-start | bytes 393224 | tf_op jit(solution)/shard_map/while/body/eval_jaxpr/ppermute | solution.py:19
  134.0 6.4 %collective-permute-start = (bf16[8,4096]{1,0:T(8,128)(2,1)S(1)}, bf16[8,4096]{1,0:T(8,128)(2,1)S(1)}, u32[]{:S(2)}, u32[]{:S(2)}) collective-permute-start(bf16[8,4096]{1,0:T(8,128)(2,1)S(1)} %get-tuple-element.210), channel_id=1, source_target_pairs={{15,0},{0,1},{1,2},{2,3},{3,4},{4,5},{5,6},{6,7},{7,8},{8,9},{9,10... | collective-permute-start | bytes 196616 | tf_op jit(solution)/shard_map/while/body/eval_jaxpr/ppermute | solution.py:19
  134.1 6.7 %collective-permute-start.1 = (f32[8,4,8]{2,0,1:T(8,128)S(1)}, f32[8,4,8]{2,0,1:T(8,128)S(1)}, u32[]{:S(2)}, u32[]{:S(2)}) collective-permute-start(f32[8,4,8]{2,0,1:T(8,128)S(1)} %get-tuple-element.211), channel_id=1, source_target_pairs={{15,0},{0,1},{1,2},{2,3},{3,4},{4,5},{5,6},{6,7},{7,8},{8,9},{9,10... | collective-permute-start | bytes 3080 | tf_op jit(solution)/shard_map/while/body/eval_jaxpr/ppermute | solution.py:19
  134.2 6.9 %collective-permute-start.3 = (f32[8,4,8]{2,0,1:T(8,128)S(1)}, f32[8,4,8]{2,0,1:T(8,128)S(1)}, u32[]{:S(2)}, u32[]{:S(2)}) collective-permute-start(f32[8,4,8]{2,0,1:T(8,128)S(1)} %get-tuple-element.212), channel_id=1, source_target_pairs={{15,0},{0,1},{1,2},{2,3},{3,4},{4,5},{5,6},{6,7},{7,8},{8,9},{9,10... | collective-permute-start | bytes 3080 | tf_op jit(solution)/shard_map/while/body/eval_jaxpr/ppermute | solution.py:19
  135.5 7.1 %collective-permute-start.4 = (f32[8,4,8,128]{3,2,0,1:T(8,128)S(1)}, f32[8,4,8,128]{3,2,0,1:T(8,128)S(1)}, u32[]{:S(2)}, u32[]{:S(2)}) collective-permute-start(f32[8,4,8,128]{3,2,0,1:T(8,128)S(1)} %get-tuple-element.214), channel_id=1, source_target_pairs={{15,0},{0,1},{1,2},{2,3},{3,4},{4,5},{5,6},{6,7},{7,8},{8,9},{9,10... | collective-permute-start | bytes 393224 | tf_op jit(solution)/shard_map/while/body/eval_jaxpr/ppermute | solution.py:19
  143.0 6.4 %collective-permute-start.5 = (bf16[8,4096]{1,0:T(8,128)(2,1)S(1)}, bf16[8,4096]{1,0:T(8,128)(2,1)S(1)}, u32[]{:S(2)}, u32[]{:S(2)}) collective-permute-start(bf16[8,4096]{1,0:T(8,128)(2,1)S(1)} %bitcast.45), channel_id=1, source_target_pairs={{15,0},{0,1},{1,2},{2,3},{3,4},{4,5},{5,6},{6,7},{7,8},{8,9},{9,10... | collective-permute-start | bytes 196616 | tf_op jit(solution)/shard_map/ppermute | solution.py:19
  (16 other events, 72.0 us)
where the time goes:
time: 150 us
  waiting for transfers between devices  103 us (69%)
  starting transfers between devices  27.2 us (18%)
  matrix products  8.33 us (6%)
  local copies, waits for them, and re-layouts  5.02 us (3%)
  other arithmetic  4.93 us (3%)
  loops' own time  1.5 us (1%)
    ppermute x76, waiting for transfers between devices, shifted(): return lax.ppermute(block, axis, route)  103 us
    ppermute x76, starting transfers between devices, shifted(): return lax.ppermute(block, axis, route)  27.2 us
    dot_general x16, matrix products, absorb_block(): jnp.einsum('rkgd,tkd->rkgt', q_heads, k_heads, preferred_element_type=jnp...  4.58 us
    dot_general x16, matrix products, absorb_block(): jnp.einsum('rkgt,tkd->rkgd', weights.astype(jnp.bfloat16), v_heads, prefe...  3.75 us
    unnamed x10, local copies, waits for them, and re-layouts  3.61 us
    reduce_sum x16, other arithmetic, absorb_block(): new_sum = run_sum * factor + jnp.sum(weights, axis=-1)  3.26 us
  transfers between devices with their start and end apart: 76, of which 47 were waited for; matrix products, arithmetic and copies ran while one was open for 6% of the time, Pallas kernels for 0%

commit v1 on v0

v1 whole, which is shorter than its diff:
```python
import functools
import math

import jax
import jax.numpy as jnp
from jax import lax
from jax.experimental import pallas as pl
from jax.experimental.pallas import tpu as pltpu
from jax.sharding import PartitionSpec as P

KV_HEADS = 4
HEAD_DIM = 128
NEGATIVE_FILL = -1e30
LOG2E = math.log2(math.e)
MESH = pl.DeviceIdType.MESH


def each(count, body):
    if count <= 4:
        for i in range(count):
            body(i)
    else:
        lax.fori_loop(0, count, lambda i, c: (body(i), c)[1], 0)


def kernel(
    groups, q_hbm, k_hbm, v_hbm, page_ref, last_ref, out_ref,
    q_in, k_in, v_in, q_pack, v_turned, meta_mine,
    q_all, k_all, v_all, meta_all, last_all, page_col,
    part_mine, part_all, lse_mine, lse_all, res, fin,
    in_sem, q_send, q_recv, m_send, m_recv, k_send, k_recv, v_send, v_recv,
    qz_send, qz_recv, mz_send, mz_recv, o_send, o_recv, l_send, l_recv, f_send, f_recv,
):
    part, me = lax.axis_index("parts"), lax.axis_index("blk")
    member, group = lax.rem(me, KV_HEADS), lax.div(me, KV_HEADS)
    rows = q_in.shape[0]
    heads = q_in.shape[1] // HEAD_DIM
    tokens = k_in.shape[0]
    per_group = heads // KV_HEADS
    block = per_group * rows

    mates = [lax.rem(member + d, KV_HEADS) for d in (2, 1, 3)]
    mate_ids = [group * KV_HEADS + m for m in mates]
    order = sorted(range(1, groups), key=lambda s: -min(s, groups - s))

    def peer(i):
        if groups <= 4:
            return lax.rem(group + order[i], groups)
        return lax.rem(group + 1 + i, groups)

    def copy(src, dst, send, recv, target):
        return pltpu.make_async_remote_copy(
            src_ref=src, dst_ref=dst, send_sem=send, recv_sem=recv,
            device_id=(part, target), device_id_type=MESH,
        )

    load_q = pltpu.make_async_copy(q_hbm, q_in, in_sem.at[0])
    load_k = pltpu.make_async_copy(k_hbm, k_in, in_sem.at[1])
    load_v = pltpu.make_async_copy(v_hbm, v_in, in_sem.at[2])
    load_q.start()
    load_k.start()
    load_v.start()

    barrier = pltpu.get_barrier_semaphore()
    for target in mate_ids:
        pl.semaphore_signal(barrier, inc=1, device_id=(part, target), device_id_type=MESH)

    def greet(i):
        target = peer(i) * KV_HEADS + member
        pl.semaphore_signal(barrier, inc=1, device_id=(part, target), device_id_type=MESH)

    each(groups - 1, greet)

    lane = lax.broadcasted_iota(jnp.int32, (1, 128), 1)
    pattern = jnp.zeros((1, 128), jnp.int32)
    for r in range(rows):
        pattern = jnp.where(lax.rem(lane, rows) == r, last_ref[r], pattern)
    meta_mine[:, :128] = pattern
    meta_mine[:, 128:] = page_ref[...]
    meta_all[member] = meta_mine[...]

    load_q.wait()
    wide = q_in[...].astype(jnp.float32)
    stacked = jnp.concatenate(
        [wide[:, h * HEAD_DIM:(h + 1) * HEAD_DIM] for h in range(heads)], axis=0
    )
    q_pack[...] = stacked.astype(jnp.bfloat16).reshape(KV_HEADS, block, HEAD_DIM)
    q_all[group, member] = q_pack[member]
    load_k.wait()

    pl.semaphore_wait(barrier, KV_HEADS - 1 + groups - 1)

    q_copies, m_copies, k_copies = [], [], []
    for i, (m, target) in enumerate(zip(mates, mate_ids)):
        q_copies.append(copy(q_pack.at[m], q_all.at[group, member], q_send.at[i], q_recv.at[member], target))
        q_copies[-1].start()
        m_copies.append(copy(meta_mine, meta_all.at[member], m_send.at[i], m_recv.at[member], target))
        m_copies[-1].start()
    for i, (m, target) in enumerate(zip(mates, mate_ids)):
        columns = pl.ds(pl.multiple_of(m * HEAD_DIM, HEAD_DIM), HEAD_DIM)
        k_copies.append(copy(k_in.at[:, columns], k_all.at[member], k_send.at[i], k_recv.at[member], target))
        k_copies[-1].start()

    load_v.wait()
    v_turned[...] = (
        v_in[...].astype(jnp.float32).T.astype(jnp.bfloat16).reshape(KV_HEADS, HEAD_DIM, tokens)
    )
    v_copies = []
    for i, (m, target) in enumerate(zip(mates, mate_ids)):
        v_copies.append(copy(v_turned.at[m], v_all.at[member], v_send.at[i], v_recv.at[member], target))
        v_copies[-1].start()

    for m, target in zip(mates, mate_ids):
        copy(q_all.at[group, m], q_all.at[group, m], q_send.at[0], q_recv.at[m], target).wait_recv()
        copy(meta_all.at[m], meta_all.at[m], m_send.at[0], m_recv.at[m], target).wait_recv()
    last_all[group] = meta_all[:, :, :128]

    def q_copy(i):
        target = peer(i) * KV_HEADS + member
        return copy(q_all.at[group], q_all.at[group], qz_send.at[i], qz_recv.at[group], target)

    def m_copy(i):
        target = peer(i) * KV_HEADS + member
        return copy(last_all.at[group], last_all.at[group], mz_send.at[i], mz_recv.at[group], target)

    def forward(i):
        m_copy(i).start()
        q_copy(i).start()

    each(groups - 1, forward)

    own = pl.ds(pl.multiple_of(member * HEAD_DIM, HEAD_DIM), HEAD_DIM)
    k_all[member] = k_in[:, own]
    v_all[member] = v_turned[member]
    for s in range(KV_HEADS):
        pages = meta_all[s][:, 128:].astype(jnp.float32)
        page_col[s] = jnp.broadcast_to(pages, (HEAD_DIM, tokens)).T

    for m, target in zip(mates, mate_ids):
        copy(k_all.at[m], k_all.at[m], k_send.at[0], k_recv.at[m], target).wait_recv()
    for m, target in zip(mates, mate_ids):
        copy(v_all.at[m], v_all.at[m], v_send.at[0], v_recv.at[m], target).wait_recv()

    factor = LOG2E / math.sqrt(HEAD_DIM)

    def attend(which):
        lasts = last_all[which].astype(jnp.float32)
        per_row = 128 // block
        pieces = []
        for first in range(0, KV_HEADS, per_row):
            piece = lasts[first]
            for k in range(1, per_row):
                piece = jnp.where(lane < k * block, piece, lasts[first + k])
            pieces.append(piece)
        last_row = jnp.concatenate(pieces, axis=1)
        queries = q_all[which].reshape(KV_HEADS * block, HEAD_DIM)
        masked = []
        for s in range(KV_HEADS):
            scores = lax.dot_general(
                k_all[s], queries, (((1,), (1,)), ((), ())), preferred_element_type=jnp.float32
            )
            column = page_col[s]
            pages = jnp.concatenate([column] * len(pieces), axis=1)
            masked.append(jnp.where(pages <= last_row, scores, NEGATIVE_FILL))
        top = functools.reduce(jnp.maximum, [jnp.max(x, axis=0, keepdims=True) for x in masked])
        total = jnp.zeros_like(top)
        out = jnp.zeros((HEAD_DIM, KV_HEADS * block), jnp.float32)
        for s in range(KV_HEADS):
            weights = jnp.exp2((masked[s] - top) * factor)
            total = total + jnp.sum(weights, axis=0, keepdims=True)
            out = out + jnp.dot(
                v_all[s], weights.astype(jnp.bfloat16), preferred_element_type=jnp.float32
            )
        return (out / total).astype(jnp.bfloat16), top * factor + jnp.log(total) * LOG2E

    def o_copy(i):
        to = peer(i)
        target = to * KV_HEADS + member
        return copy(part_mine.at[to], part_all.at[group], o_send.at[i], o_recv.at[group], target)

    def l_copy(i):
        to = peer(i)
        target = to * KV_HEADS + member
        return copy(lse_mine.at[to], lse_all.at[group], l_send.at[i], l_recv.at[group], target)

    def work(i):
        other = peer(i)
        target = other * KV_HEADS + member
        copy(last_all.at[other], last_all.at[other], mz_send.at[0], mz_recv.at[other], target).wait_recv()
        copy(q_all.at[other], q_all.at[other], qz_send.at[0], qz_recv.at[other], target).wait_recv()
        out, lse = attend(other)
        part_mine[other] = out
        lse_mine[other] = lse
        l_copy(i).start()
        o_copy(i).start()

    each(groups - 1, work)
    out, lse = attend(group)
    part_all[group] = out
    lse_all[group] = lse

    def arrive(i):
        other = peer(i)
        target = other * KV_HEADS + member
        copy(lse_all.at[other], lse_all.at[other], l_send.at[0], l_recv.at[other], target).wait_recv()
        copy(part_all.at[other], part_all.at[other], o_send.at[0], o_recv.at[other], target).wait_recv()

    each(groups - 1, arrive)

    def loop(body, start):
        if groups <= 4:
            for i in range(groups):
                start = body(i, start)
            return start
        return lax.fori_loop(0, groups, body, start)

    top = loop(lambda i, t: jnp.maximum(t, lse_all[i]), jnp.full((1, KV_HEADS * block), NEGATIVE_FILL, jnp.float32))

    def merge(i, carry):
        total, acc = carry
        share = jnp.exp2(lse_all[i] - top)
        return total + share, acc + share * part_all[i].astype(jnp.float32)

    total, acc = loop(
        merge,
        (jnp.zeros((1, KV_HEADS * block), jnp.float32), jnp.zeros((HEAD_DIM, KV_HEADS * block), jnp.float32)),
    )
    res[...] = (acc / total).T.astype(jnp.bfloat16).reshape(KV_HEADS, block, HEAD_DIM)

    f_copies = []
    for i, (m, target) in enumerate(zip(mates, mate_ids)):
        f_copies.append(copy(res.at[m], fin.at[member], f_send.at[i], f_recv.at[member], target))
        f_copies[-1].start()
    fin[member] = res[member]
    for m, target in zip(mates, mate_ids):
        copy(fin.at[m], fin.at[m], f_send.at[0], f_recv.at[m], target).wait_recv()
    for s in range(KV_HEADS):
        done = fin[s].astype(jnp.float32)
        line = jnp.concatenate([done[h * rows:(h + 1) * rows] for h in range(per_group)], axis=1)
        width = per_group * HEAD_DIM
        out_ref[:, s * width:(s + 1) * width] = line.astype(jnp.bfloat16)

    for c in q_copies + m_copies + k_copies + v_copies + f_copies:
        c.wait_send()

    def drain(i):
        m_copy(i).wait_send()
        q_copy(i).wait_send()
        l_copy(i).wait_send()
        o_copy(i).wait_send()

    each(groups - 1, drain)


def shards(queries, key_cache, value_cache, tile_page, row_last):
    groups = lax.axis_size("blk") // KV_HEADS
    rows, width = queries.shape
    tokens = key_cache.shape[0]
    block = width // HEAD_DIM // KV_HEADS * rows
    bf16, f32 = jnp.bfloat16, jnp.float32
    dma = pltpu.SemaphoreType.DMA
    quad, far = dma((KV_HEADS,)), dma((groups,))
    return pl.pallas_call(
        functools.partial(kernel, groups),
        out_shape=jax.ShapeDtypeStruct((rows, width), bf16),
        in_specs=[pl.BlockSpec(memory_space=pl.ANY)] * 3
        + [pl.BlockSpec(memory_space=pltpu.VMEM), pl.BlockSpec(memory_space=pltpu.SMEM)],
        out_specs=pl.BlockSpec(memory_space=pltpu.VMEM),
        scratch_shapes=[
            pltpu.VMEM((rows, width), bf16),
            pltpu.VMEM(key_cache.shape, bf16),
            pltpu.VMEM(value_cache.shape, bf16),
            pltpu.VMEM((KV_HEADS, block, HEAD_DIM), bf16),
            pltpu.VMEM((KV_HEADS, HEAD_DIM, tokens), bf16),
            pltpu.VMEM((1, 128 + tokens), jnp.int32),
            pltpu.VMEM((groups, KV_HEADS, block, HEAD_DIM), bf16),
            pltpu.VMEM((KV_HEADS, tokens, HEAD_DIM), bf16),
            pltpu.VMEM((KV_HEADS, HEAD_DIM, tokens), bf16),
            pltpu.VMEM((KV_HEADS, 1, 128 + tokens), jnp.int32),
            pltpu.VMEM((groups, KV_HEADS, 1, 128), jnp.int32),
            pltpu.VMEM((KV_HEADS, tokens, HEAD_DIM), f32),
            pltpu.VMEM((groups, HEAD_DIM, KV_HEADS * block), bf16),
            pltpu.VMEM((groups, HEAD_DIM, KV_HEADS * block), bf16),
            pltpu.VMEM((groups, 1, KV_HEADS * block), f32),
            pltpu.VMEM((groups, 1, KV_HEADS * block), f32),
            pltpu.VMEM((KV_HEADS, block, HEAD_DIM), bf16),
            pltpu.VMEM((KV_HEADS, block, HEAD_DIM), bf16),
            dma((3,)),
            *([quad] * 8),
            *([far] * 8),
            *([quad] * 2),
        ],
        compiler_params=pltpu.CompilerParams(
            collective_id=0, has_side_effects=True, vmem_limit_bytes=40 * 1024 * 1024
        ),
        cost_estimate=pl.CostEstimate(flops=540_000_000, bytes_accessed=700_000, transcendentals=1_000_000),
    )(queries, key_cache, value_cache, tile_page.reshape(1, tokens), row_last)


def solution(mesh):
    placed = (
        P(("parts", "blk"), None),
        P(("parts", "blk"), None),
        P(("parts", "blk"), None),
        P(("parts", "blk")),
        P(("parts", "blk")),
    )
    return jax.shard_map(
        shards, mesh=mesh, in_specs=placed, out_specs=P(("parts", "blk"), None), check_vma=False
    )
```

time: 150 us -> 30 us (0.20)
  waiting for transfers between devices: 103 us -> 0 us
  starting transfers between devices: 27.2 us -> 0 us
  Pallas kernels: 0 us -> 25.7 us
  matrix products: 8.33 us -> 0 us
  other arithmetic: 4.93 us -> 0 us
  loops' own time: 1.5 us -> 0 us
    ppermute x76 -> x0, waiting for transfers between devices: 103 us -> none  [shifted(): return lax.ppermute(block, axis, route)]
    ppermute x76 -> x0, starting transfers between devices: 27.2 us -> none  [shifted(): return lax.ppermute(block, axis, route)]
    pallas_call x0 -> x1, Pallas kernels: none -> 25.7 us  [shards(): pl.pallas_call(functools.partial(kernel, groups), out_shape=jax.ShapeDtyp...]
    dot_general x32 -> x0, matrix products: 8.33 us -> none  [the longest x16 4.58 us: absorb_block(): jnp.einsum('rkgd,tkd->rkgt', q_heads, k_heads, preferred_element_type=jnp...]
    reduce_sum x16 -> x0, other arithmetic: 3.26 us -> none  [absorb_block(): new_sum = run_sum * factor + jnp.sum(weights, axis=-1)]
    another operation x1 -> x0, loops' own time: 1.5 us -> none  [shards(): final_pair = lax.fori_loop(0, blocks - 1, turn, (own_rows, carried))]
    unnamed x10 -> x11, local copies, waits for them, and re-layouts: 3.61 us -> 4.06 us
  transfers between devices with their start and end apart: 76 -> 0, of which waited for: 47 -> 0; matrix products, arithmetic and copies ran while one was open for 6% -> 0% of each run, Pallas kernels for 0% -> 0%
where the time goes in v1:
time: 30 us; the launch traced here: 29.8 us
  Pallas kernels  25.7 us (86%)
  local copies, waits for them, and re-layouts  4.06 us (14%)
    pallas_call x1, Pallas kernels, shards(): pl.pallas_call(functools.partial(kernel, groups), out_shape=jax.ShapeDtyp...  25.7 us
    unnamed x11, local copies, waits for them, and re-layouts  4.06 us

profile of v1, /device:TPU:0, one launch (start us, length us, event | category | flops | bytes accessed | tf_op | source)
XLA Modules:
  0.0 29.8 jit_solution(15147982655054239451)
XLA Ops:
  0.0 0.0 copy-start.4
  0.0 0.0 copy-start.3
  0.0 0.7 %copy-done.4 = s32[8]{0:T(128)S(1)} copy-done((s32[8]{0:T(128)S(1)}, s32[8]{0:T(128)}, u32[]{:S(2)}) %copy-start.4) | copy-done | bytes 56
  0.7 0.0 copy-done.3
  0.7 0.0 copy-start
  0.7 0.9 %copy-done = bf16[256,512]{1,0:T(8,128)(2,1)S(1)} copy-done((bf16[256,512]{1,0:T(8,128)(2,1)S(1)}, bf16[256,512]{1,0:T(8,128)(2,1)}, u32[]{:S(2)}) %copy-start) | copy-done | bytes 262168
  1.6 0.0 copy-start.1
  1.6 0.9 %copy-done.1 = bf16[256,512]{1,0:T(8,128)(2,1)S(1)} copy-done((bf16[256,512]{1,0:T(8,128)(2,1)S(1)}, bf16[256,512]{1,0:T(8,128)(2,1)}, u32[]{:S(2)}) %copy-start.1) | copy-done | bytes 262168
  2.6 0.0 copy-start.2
  2.6 0.8 %copy-done.2 = bf16[8,4096]{1,0:T(8,128)(2,1)S(1)} copy-done((bf16[8,4096]{1,0:T(8,128)(2,1)S(1)}, bf16[8,4096]{1,0:T(8,128)(2,1)}, u32[]{:S(2)}) %copy-start.2) | copy-done | bytes 65560
  3.4 25.7 %shard_map.55 = bf16[8,4096]{1,0:T(8,128)(2,1)S(1)} custom-call(bf16[8,4096]{1,0:T(8,128)(2,1)S(1)} %copy-done.2, bf16[256,512]{1,0:T(8,128)(2,1)S(1)} %copy-done, bf16[256,512]{1,0:T(8,128)(2,1)S(1)} %copy-done.1, s32[1,256]{1,0:T(1,128)S(1)} %bitcast.1, s32[8]{0:T(128)S(1)} %copy-done.4), custom_call_target="tpu_custom_call" | custom-call | flops 540000000 | bytes 700000 | tf_op jit(solution)/shard_map/pallas_call | solution.py:263
  29.2 0.6 %copy.7 = bf16[8,4096]{1,0:T(8,128)(2,1)} copy(bf16[8,4096]{1,0:T(8,128)(2,1)S(1)} %shard_map.55) | data formatting | bytes 131072
Async XLA Ops:
  0.0 0.7 %copy-start.4 = (s32[8]{0:T(128)S(1)}, s32[8]{0:T(128)}, u32[]{:S(2)}) copy-start(s32[8]{0:T(128)} %last_ref.1) | copy-start | bytes 100
  0.0 0.7 %copy-start.3 = (s32[256]{0:T(256)S(1)}, s32[256]{0:T(256)}, u32[]{:S(2)}) copy-start(s32[256]{0:T(256)} %param.8) | copy-start | bytes 3076
  0.7 0.9 %copy-start = (bf16[256,512]{1,0:T(8,128)(2,1)S(1)}, bf16[256,512]{1,0:T(8,128)(2,1)}, u32[]{:S(2)}) copy-start(bf16[256,512]{1,0:T(8,128)(2,1)} %k_hbm.1) | copy-start | bytes 786436
  1.6 0.9 %copy-start.1 = (bf16[256,512]{1,0:T(8,128)(2,1)S(1)}, bf16[256,512]{1,0:T(8,128)(2,1)}, u32[]{:S(2)}) copy-start(bf16[256,512]{1,0:T(8,128)(2,1)} %v_hbm.1) | copy-start | bytes 786436
  2.6 0.8 %copy-start.2 = (bf16[8,4096]{1,0:T(8,128)(2,1)S(1)}, bf16[8,4096]{1,0:T(8,128)(2,1)}, u32[]{:S(2)}) copy-start(bf16[8,4096]{1,0:T(8,128)(2,1)} %q_hbm.1) | copy-start | bytes 196612

commit v2 on v0

v2 whole, which is shorter than its diff:
```python
import functools
import math

import jax
import jax.numpy as jnp
from jax import lax
from jax.experimental import pallas as pl
from jax.experimental.pallas import tpu as pltpu
from jax.sharding import PartitionSpec as P

KV_HEADS = 4
HEAD_DIM = 128
NEGATIVE_FILL = -1e30
LOG2E = math.log2(math.e)
MESH = pl.DeviceIdType.MESH


def each(count, body):
    if count <= 15:
        for i in range(count):
            body(i)
    else:
        lax.fori_loop(0, count, lambda i, c: (body(i), c)[1], 0)


def kernel(
    groups, q_hbm, k_hbm, v_hbm, page_hbm, last_hbm, out_ref,
    q_in, last_in, q_pack, last_mine, q_all, k_all, v_all, v_turned, page_all, last_all, page_col,
    part_mine, part_all, lse_mine, lse_all,
    in_sem, own_sem, q_send, q_recv, qz_send, k_send, k_recv, v_send, v_recv,
    page_send, page_recv, last_send, last_recv, o_send, o_recv, l_send, l_recv,
):
    part, me = lax.axis_index("parts"), lax.axis_index("blk")
    member, group = lax.rem(me, KV_HEADS), lax.div(me, KV_HEADS)
    blocks = groups * KV_HEADS
    rows = q_in.shape[0]
    heads = q_in.shape[1] // HEAD_DIM
    tokens = k_all.shape[1]
    per_group = heads // KV_HEADS
    block = per_group * rows

    twin = member + 1 - 2 * lax.rem(member, 2)
    across = [lax.rem(member + 2, KV_HEADS), lax.rem(twin + 2, KV_HEADS)]
    mates = across + [twin]
    mate_ids = [group * KV_HEADS + m for m in mates]
    order = sorted(range(1, groups), key=lambda s: -min(s, groups - s))

    def peer(i):
        if groups <= 4:
            return lax.rem(group + order[i], groups)
        return lax.rem(group + 1 + i, groups)

    def copy(src, dst, send, recv, target):
        return pltpu.make_async_remote_copy(
            src_ref=src, dst_ref=dst, send_sem=send, recv_sem=recv,
            device_id=(part, target), device_id_type=MESH,
        )

    own = pl.ds(pl.multiple_of(member * HEAD_DIM, HEAD_DIM), HEAD_DIM)
    load_q = pltpu.make_async_copy(q_hbm, q_in, in_sem.at[0])
    load_last = pltpu.make_async_copy(last_hbm, last_in, in_sem.at[1])
    load_k = pltpu.make_async_copy(k_hbm.at[:, own], k_all.at[member], own_sem.at[0])
    load_v = pltpu.make_async_copy(v_hbm.at[:, own], v_all.at[member], own_sem.at[1])
    load_page = pltpu.make_async_copy(page_hbm, page_all.at[member], own_sem.at[2])
    load_q.start()
    load_last.start()

    barrier = pltpu.get_barrier_semaphore()

    def others(body):
        each(blocks - 1, lambda i: body(lax.rem(me + 1 + i, blocks)))

    def greet(target):
        pl.semaphore_signal(barrier, inc=1, device_id=(part, target), device_id_type=MESH)

    others(greet)
    load_k.start()
    load_v.start()
    load_page.start()

    load_q.wait()
    wide = q_in[...].astype(jnp.float32)
    stacked = jnp.concatenate(
        [wide[:, h * HEAD_DIM:(h + 1) * HEAD_DIM] for h in range(heads)], axis=0
    )
    q_pack[...] = stacked.astype(jnp.bfloat16).reshape(KV_HEADS, block, HEAD_DIM)
    q_all[group, member] = q_pack[member]

    load_last.wait()
    lane = lax.broadcasted_iota(jnp.int32, (1, 128), 1)
    pattern = jnp.zeros((1, 128), jnp.int32)
    for r in range(rows):
        pattern = jnp.where(lax.rem(lane, rows) == r, last_in[r], pattern)
    last_mine[...] = pattern
    last_all[me] = pattern

    pl.semaphore_wait(barrier, blocks - 1)

    q_copies = []
    for i, (m, target) in enumerate(zip(mates, mate_ids)):
        q_copies.append(copy(q_pack.at[m], q_all.at[group, member], q_send.at[i], q_recv.at[me], target))
        q_copies[-1].start()

    def direct(i, k):
        m = (member, twin)[k]
        return copy(
            q_pack.at[m], q_all.at[group, member], qz_send.at[peer(i), k], q_recv.at[me],
            peer(i) * KV_HEADS + m,
        )

    def relay(i, k):
        m = across[k]
        return copy(
            q_all.at[group, m], q_all.at[group, m], qz_send.at[peer(i), 2 + k],
            q_recv.at[group * KV_HEADS + m], peer(i) * KV_HEADS + member,
        )

    def send_direct(i):
        direct(i, 0).start()
        direct(i, 1).start()

    each(groups - 1, send_direct)

    kv_copies = []
    for i, (m, target) in enumerate(zip(mates, mate_ids)):
        columns = pl.ds(pl.multiple_of(m * HEAD_DIM, HEAD_DIM), HEAD_DIM)
        kv_copies.append(copy(k_hbm.at[:, columns], k_all.at[member], k_send.at[i], k_recv.at[member], target))
        kv_copies[-1].start()

    def q_wait(index):
        g, m = lax.div(index, KV_HEADS), lax.rem(index, KV_HEADS)
        copy(q_all.at[g, m], q_all.at[g, m], q_send.at[0], q_recv.at[index], mate_ids[0]).wait_recv()

    q_wait(mate_ids[0])
    q_wait(mate_ids[1])

    def send_relay(i):
        relay(i, 0).start()
        relay(i, 1).start()

    each(groups - 1, send_relay)

    for i, (m, target) in enumerate(zip(mates, mate_ids)):
        columns = pl.ds(pl.multiple_of(m * HEAD_DIM, HEAD_DIM), HEAD_DIM)
        copy(page_hbm, page_all.at[member], page_send, page_recv, target).start()
        kv_copies.append(copy(v_hbm.at[:, columns], v_all.at[member], v_send.at[i], v_recv.at[member], target))
        kv_copies[-1].start()
    others(lambda t: copy(last_mine, last_all.at[me], last_send, last_recv, t).start())

    few = pl.ds(0, KV_HEADS - 1)
    page_wait = copy(page_all.at[few], page_all.at[few], page_send, page_recv, mate_ids[0])
    rest = pl.ds(0, blocks - 1)
    last_wait = copy(last_all.at[rest], last_all.at[rest], last_send, last_recv, mate_ids[0])
    load_page.wait()
    page_wait.wait_recv()
    for s in range(KV_HEADS):
        pages = page_all[s].astype(jnp.float32)
        page_col[s] = jnp.broadcast_to(pages, (HEAD_DIM, tokens)).T

    factor = LOG2E / math.sqrt(HEAD_DIM)

    def weigh(which):
        per_row = 128 // block
        pieces = []
        for first in range(0, KV_HEADS, per_row):
            piece = last_all[which * KV_HEADS + first]
            for k in range(1, per_row):
                piece = jnp.where(lane < k * block, piece, last_all[which * KV_HEADS + first + k])
            pieces.append(piece)
        last_row = jnp.concatenate(pieces, axis=1).astype(jnp.float32)
        queries = q_all[which].reshape(KV_HEADS * block, HEAD_DIM)
        masked = []
        for s in range(KV_HEADS):
            scores = lax.dot_general(
                k_all[s], queries, (((1,), (1,)), ((), ())), preferred_element_type=jnp.float32
            )
            pages = jnp.concatenate([page_col[s]] * len(pieces), axis=1)
            masked.append(jnp.where(pages <= last_row, scores, NEGATIVE_FILL))
        top = functools.reduce(jnp.maximum, [jnp.max(x, axis=0, keepdims=True) for x in masked])
        total = jnp.zeros_like(top)
        rounded = []
        for s in range(KV_HEADS):
            weights = jnp.exp2((masked[s] - top) * factor)
            total = total + jnp.sum(weights, axis=0, keepdims=True)
            rounded.append(weights.astype(jnp.bfloat16))
        return rounded, total, top * factor + jnp.log(total) * LOG2E

    def attend(weighed):
        rounded, total, lse = weighed
        out = jnp.zeros((HEAD_DIM, KV_HEADS * block), jnp.float32)
        for s in range(KV_HEADS):
            out = out + jnp.dot(v_turned[s], rounded[s], preferred_element_type=jnp.float32)
        out = (out / total).T.astype(jnp.bfloat16).reshape(KV_HEADS, block, HEAD_DIM)
        return out, lse

    def far_weigh(i):
        for m in range(KV_HEADS):
            q_wait(peer(i) * KV_HEADS + m)
        return weigh(peer(i))

    def send_out(index):
        copy(lse_mine.at[index], lse_all.at[me], l_send, l_recv, index).start()
        copy(part_mine.at[index], part_all.at[me], o_send, o_recv, index).start()

    def far_attend(i, weighed):
        out, lse = attend(weighed)
        base = peer(i) * KV_HEADS
        part_mine[pl.ds(base, KV_HEADS)] = out
        for m in range(KV_HEADS):
            first = m * block // 128 * 128
            lse_mine[base + m] = lse[:, first:first + 128]
        for m in range(KV_HEADS):
            send_out(base + m)

    q_wait(mate_ids[2])
    load_k.wait()
    for m, target in zip(mates, mate_ids):
        copy(k_all.at[m], k_all.at[m], k_send.at[0], k_recv.at[m], target).wait_recv()
    last_wait.wait_recv()
    own_weighed = weigh(group)
    first_weighed = far_weigh(0)

    load_v.wait()
    for m, target in zip(mates, mate_ids):
        copy(v_all.at[m], v_all.at[m], v_send.at[0], v_recv.at[m], target).wait_recv()
    for s in range(KV_HEADS):
        v_turned[s] = v_all[s].astype(jnp.float32).T.astype(jnp.bfloat16)

    far_attend(0, first_weighed)
    each(groups - 2, lambda i: far_attend(i + 1, far_weigh(i + 1)))
    out, lse = attend(own_weighed)
    base = group * KV_HEADS
    part_mine[pl.ds(base, KV_HEADS)] = out
    for m in range(KV_HEADS):
        first = m * block // 128 * 128
        lse_mine[base + m] = lse[:, first:first + 128]
    for target in mate_ids:
        send_out(target)
    part_all[me] = part_mine[me]
    lse_all[me] = lse_mine[me]

    lse_wait = copy(lse_all.at[rest], lse_all.at[rest], l_send, l_recv, mate_ids[0])
    out_wait = copy(part_all.at[rest], part_all.at[rest], o_send, o_recv, mate_ids[0])
    lse_wait.wait_recv()
    shares = [None] * blocks
    for m in range(KV_HEADS):
        found = [lse_all[g * KV_HEADS + m] for g in range(groups)]
        top = functools.reduce(jnp.maximum, found)
        found = [jnp.exp2(x - top) for x in found]
        total = functools.reduce(jnp.add, found)
        for g in range(groups):
            shares[g * KV_HEADS + m] = found[g] / total
    if blocks < 128:
        shares.append(jnp.zeros((128 - blocks, 128), jnp.float32))
    turned = jnp.concatenate(shares, axis=0).T
    place = lax.rem(member, 128 // block)
    columns = turned[:block]
    for k in range(1, 128 // block):
        columns = jnp.where(place == k, turned[k * block:(k + 1) * block], columns)

    out_wait.wait_recv()
    for m in range(KV_HEADS):
        done = jnp.zeros((block, HEAD_DIM), jnp.float32)
        for g in range(groups):
            source = g * KV_HEADS + m
            done = done + columns[:, source:source + 1] * part_all[source].astype(jnp.float32)
        line = jnp.concatenate([done[h * rows:(h + 1) * rows] for h in range(per_group)], axis=1)
        width = per_group * HEAD_DIM
        out_ref[:, m * width:(m + 1) * width] = line.astype(jnp.bfloat16)

    for c in q_copies + kv_copies:
        c.wait_send()

    def drain(i):
        for k in range(2):
            direct(i, k).wait_send()
            relay(i, k).wait_send()

    each(groups - 1, drain)
    page_wait.wait_send()
    last_wait.wait_send()
    lse_wait.wait_send()
    out_wait.wait_send()


def shards(queries, key_cache, value_cache, tile_page, row_last):
    groups = lax.axis_size("blk") // KV_HEADS
    blocks = lax.axis_size("blk")
    rows, width = queries.shape
    tokens = key_cache.shape[0]
    block = width // HEAD_DIM // KV_HEADS * rows
    bf16, f32 = jnp.bfloat16, jnp.float32
    dma = pltpu.SemaphoreType.DMA
    quad, one = dma((KV_HEADS,)), dma
    return pl.pallas_call(
        functools.partial(kernel, groups),
        out_shape=jax.ShapeDtypeStruct((rows, width), bf16),
        in_specs=[pl.BlockSpec(memory_space=pltpu.HBM)] * 5,
        out_specs=pl.BlockSpec(memory_space=pltpu.VMEM),
        scratch_shapes=[
            pltpu.VMEM((rows, width), bf16),
            pltpu.SMEM((rows,), jnp.int32),
            pltpu.VMEM((KV_HEADS, block, HEAD_DIM), bf16),
            pltpu.VMEM((1, 128), jnp.int32),
            pltpu.VMEM((groups, KV_HEADS, block, HEAD_DIM), bf16),
            pltpu.VMEM((KV_HEADS, tokens, HEAD_DIM), bf16),
            pltpu.VMEM((KV_HEADS, tokens, HEAD_DIM), bf16),
            pltpu.VMEM((KV_HEADS, HEAD_DIM, tokens), bf16),
            pltpu.VMEM((KV_HEADS, 1, tokens), jnp.int32),
            pltpu.VMEM((blocks, 1, 128), jnp.int32),
            pltpu.VMEM((KV_HEADS, tokens, HEAD_DIM), f32),
            pltpu.VMEM((blocks, block, HEAD_DIM), bf16),
            pltpu.VMEM((blocks, block, HEAD_DIM), bf16),
            pltpu.VMEM((blocks, 1, 128), f32),
            pltpu.VMEM((blocks, 1, 128), f32),
            dma((2,)), dma((3,)),
            quad, dma((blocks,)), dma((groups, 4)), quad, quad, quad, quad,
            one, one, one, one, one, one, one, one,
        ],
        compiler_params=pltpu.CompilerParams(
            collective_id=0, has_side_effects=True, vmem_limit_bytes=60 * 1024 * 1024
        ),
        cost_estimate=pl.CostEstimate(flops=540_000_000, bytes_accessed=700_000, transcendentals=1_000_000),
    )(queries, key_cache, value_cache, tile_page.reshape(1, tokens), row_last)


def solution(mesh):
    placed = (
        P(("parts", "blk"), None),
        P(("parts", "blk"), None),
        P(("parts", "blk"), None),
        P(("parts", "blk")),
        P(("parts", "blk")),
    )
    return jax.shard_map(
        shards, mesh=mesh, in_specs=placed, out_specs=P(("parts", "blk"), None), check_vma=False
    )
```

time: 150 us -> 24.7 us (0.16)
  waiting for transfers between devices: 103 us -> 0 us
  starting transfers between devices: 27.2 us -> 0 us
  Pallas kernels: 0 us -> 23 us
  matrix products: 8.33 us -> 0 us
  other arithmetic: 4.93 us -> 0 us
  local copies, waits for them, and re-layouts: 5.02 us -> 1.47 us
  loops' own time: 1.5 us -> 0 us
    ppermute x76 -> x0, waiting for transfers between devices: 103 us -> none  [shifted(): return lax.ppermute(block, axis, route)]
    ppermute x76 -> x0, starting transfers between devices: 27.2 us -> none  [shifted(): return lax.ppermute(block, axis, route)]
    pallas_call x0 -> x1, Pallas kernels: none -> 23 us  [shards(): pl.pallas_call(functools.partial(kernel, groups), out_shape=jax.ShapeDtyp...]
    dot_general x32 -> x0, matrix products: 8.33 us -> none  [the longest x16 4.58 us: absorb_block(): jnp.einsum('rkgd,tkd->rkgt', q_heads, k_heads, preferred_element_type=jnp...]
    reduce_sum x16 -> x0, other arithmetic: 3.26 us -> none  [absorb_block(): new_sum = run_sum * factor + jnp.sum(weights, axis=-1)]
    unnamed x10 -> x1, local copies, waits for them, and re-layouts: 3.61 us -> 1.47 us
    another operation x1 -> x0, loops' own time: 1.5 us -> none  [shards(): final_pair = lax.fori_loop(0, blocks - 1, turn, (own_rows, carried))]
  transfers between devices with their start and end apart: 76 -> 0, of which waited for: 47 -> 0; matrix products, arithmetic and copies ran while one was open for 6% -> 0% of each run, Pallas kernels for 0% -> 0%
where the time goes in v2:
time: 24.7 us; the launch traced here: 24.5 us
  Pallas kernels  23 us (93%)
  local copies, waits for them, and re-layouts  1.47 us (6%)
    pallas_call x1, Pallas kernels, shards(): pl.pallas_call(functools.partial(kernel, groups), out_shape=jax.ShapeDtyp...  23 us
    unnamed x1, local copies, waits for them, and re-layouts  1.47 us

profile of v2, /device:TPU:0, one launch (start us, length us, event | category | flops | bytes accessed | tf_op | source)
XLA Modules:
  0.0 24.5 jit_solution(15969274147594187859)
XLA Ops:
  0.0 23.0 %shard_map.55 = bf16[8,4096]{1,0:T(8,128)(2,1)} custom-call(bf16[8,4096]{1,0:T(8,128)(2,1)} %q_hbm.1, bf16[256,512]{1,0:T(8,128)(2,1)} %k_hbm.1, bf16[256,512]{1,0:T(8,128)(2,1)} %v_hbm.1, s32[1,256]{1,0:T(1,128)} %bitcast.1, s32[8]{0:T(128)} %last_hbm.1), custom_call_target="tpu_custom_call" | custom-call | flops 540000000 | bytes 700000 | tf_op jit(solution)/shard_map/pallas_call | solution.py:295
  23.0 1.5 %copy.7 = bf16[8,4096]{1,0:T(8,128)(2,1)} copy(bf16[8,4096]{1,0:T(8,128)(2,1)} %shard_map.55) | data formatting | bytes 131072

commit v3 on v2

--- a/solution.py
+++ b/solution.py
@@ -13,6 +13,7 @@
 NEGATIVE_FILL = -1e30
 LOG2E = math.log2(math.e)
 MESH = pl.DeviceIdType.MESH
+AHEAD = 2
 
 
 def each(count, body):
@@ -25,8 +26,8 @@
 
 def kernel(
     groups, q_hbm, k_hbm, v_hbm, page_hbm, last_hbm, out_ref,
-    q_in, last_in, q_pack, last_mine, q_all, k_all, v_all, v_turned, page_all, last_all, page_col,
-    part_mine, part_all, lse_mine, lse_all,
+    q_in, v_in, last_in, q_pack, last_mine, q_all, k_all, v_mine, v_all, page_all, last_all, page_col,
+    part_mine, part_all, lse_mine, lse_all, share_ref,
     in_sem, own_sem, q_send, q_recv, qz_send, k_send, k_recv, v_send, v_recv,
     page_send, page_recv, last_send, last_recv, o_send, o_recv, l_send, l_recv,
 ):
@@ -50,6 +51,11 @@
             return lax.rem(group + order[i], groups)
         return lax.rem(group + 1 + i, groups)
 
+    def source_at(i):
+        if groups <= 4:
+            return lax.rem(group + groups - order[i], groups)
+        return lax.rem(group + groups - 1 - i, groups)
+
     def copy(src, dst, send, recv, target):
         return pltpu.make_async_remote_copy(
             src_ref=src, dst_ref=dst, send_sem=send, recv_sem=recv,
@@ -60,7 +66,7 @@
     load_q = pltpu.make_async_copy(q_hbm, q_in, in_sem.at[0])
     load_last = pltpu.make_async_copy(last_hbm, last_in, in_sem.at[1])
     load_k = pltpu.make_async_copy(k_hbm.at[:, own], k_all.at[member], own_sem.at[0])
-    load_v = pltpu.make_async_copy(v_hbm.at[:, own], v_all.at[member], own_sem.at[1])
+    load_v = pltpu.make_async_copy(v_hbm, v_in, own_sem.at[1])
     load_page = pltpu.make_async_copy(page_hbm, page_all.at[member], own_sem.at[2])
     load_q.start()
     load_last.start()
@@ -131,6 +137,15 @@
         g, m = lax.div(index, KV_HEADS), lax.rem(index, KV_HEADS)
         copy(q_all.at[g, m], q_all.at[g, m], q_send.at[0], q_recv.at[index], mate_ids[0]).wait_recv()
 
+    load_v.wait()
+    v_mine[...] = (
+        v_in[...].astype(jnp.float32).T.astype(jnp.bfloat16).reshape(KV_HEADS, HEAD_DIM, tokens)
+    )
+    for i, (m, target) in enumerate(zip(mates, mate_ids)):
+        kv_copies.append(copy(v_mine.at[m], v_all.at[member], v_send.at[i], v_recv.at[member], target))
+        kv_copies[-1].start()
+    v_all[member] = v_mine[member]
+
     q_wait(mate_ids[0])
     q_wait(mate_ids[1])
 
@@ -140,11 +155,8 @@
 
     each(groups - 1, send_relay)
 
-    for i, (m, target) in enumerate(zip(mates, mate_ids)):
-        columns = pl.ds(pl.multiple_of(m * HEAD_DIM, HEAD_DIM), HEAD_DIM)
+    for target in mate_ids:
         copy(page_hbm, page_all.at[member], page_send, page_recv, target).start()
-        kv_copies.append(copy(v_hbm.at[:, columns], v_all.at[member], v_send.at[i], v_recv.at[member], target))
-        kv_copies[-1].start()
     others(lambda t: copy(last_mine, last_all.at[me], last_send, last_recv, t).start())
 
     few = pl.ds(0, KV_HEADS - 1)
@@ -186,29 +198,35 @@
         return rounded, total, top * factor + jnp.log(total) * LOG2E
 
     def attend(weighed):
-        rounded, total, lse = weighed
+        rounded, total = weighed
         out = jnp.zeros((HEAD_DIM, KV_HEADS * block), jnp.float32)
         for s in range(KV_HEADS):
-            out = out + jnp.dot(v_turned[s], rounded[s], preferred_element_type=jnp.float32)
-        out = (out / total).T.astype(jnp.bfloat16).reshape(KV_HEADS, block, HEAD_DIM)
-        return out, lse
-
-    def far_weigh(i):
-        for m in range(KV_HEADS):
-            q_wait(peer(i) * KV_HEADS + m)
-        return weigh(peer(i))
-
-    def send_out(index):
-        copy(lse_mine.at[index], lse_all.at[me], l_send, l_recv, index).start()
-        copy(part_mine.at[index], part_all.at[me], o_send, o_recv, index).start()
-
-    def far_attend(i, weighed):
-        out, lse = attend(weighed)
-        base = peer(i) * KV_HEADS
-        part_mine[pl.ds(base, KV_HEADS)] = out
+            out = out + jnp.dot(v_all[s], rounded[s], preferred_element_type=jnp.float32)
+        out = (out * (1.0 / total)).T.astype(jnp.bfloat16).reshape(KV_HEADS, block, HEAD_DIM)
+        return out
+
+    def share_lse(which, lse):
+        base = which * KV_HEADS
         for m in range(KV_HEADS):
             first = m * block // 128 * 128
             lse_mine[base + m] = lse[:, first:first + 128]
+
+    def far_weigh(i):
+        base = peer(i) * KV_HEADS
+        for m in range(KV_HEADS):
+            q_wait(base + m)
+        rounded, total, lse = weigh(peer(i))
+        share_lse(peer(i), lse)
+        for m in range(KV_HEADS):
+            copy(lse_mine.at[base + m], lse_all.at[me], l_send, l_recv, base + m).start()
+        return rounded, total
+
+    def send_out(index):
+        copy(part_mine.at[index], part_all.at[me], o_send, o_recv.at[group], index).start()
+
+    def far_attend(i, weighed):
+        base = peer(i) * KV_HEADS
+        part_mine[pl.ds(base, KV_HEADS)] = attend(weighed)
         for m in range(KV_HEADS):
             send_out(base + m)
 
@@ -217,30 +235,27 @@
     for m, target in zip(mates, mate_ids):
         copy(k_all.at[m], k_all.at[m], k_send.at[0], k_recv.at[m], target).wait_recv()
     last_wait.wait_recv()
-    own_weighed = weigh(group)
-    first_weighed = far_weigh(0)
-
-    load_v.wait()
+    rounded, total, lse = weigh(group)
+    own_weighed = rounded, total
+    share_lse(group, lse)
+    for target in mate_ids:
+        copy(lse_mine.at[target], lse_all.at[me], l_send, l_recv, target).start()
+    lse_all[me] = lse_mine[me]
+    ahead = [far_weigh(i) for i in range(min(AHEAD, groups - 1))]
+
     for m, target in zip(mates, mate_ids):
         copy(v_all.at[m], v_all.at[m], v_send.at[0], v_recv.at[m], target).wait_recv()
-    for s in range(KV_HEADS):
-        v_turned[s] = v_all[s].astype(jnp.float32).T.astype(jnp.bfloat16)
-
-    far_attend(0, first_weighed)
-    each(groups - 2, lambda i: far_attend(i + 1, far_weigh(i + 1)))
-    out, lse = attend(own_weighed)
+
+    for i, weighed in enumerate(ahead):
+        far_attend(i, weighed)
+    each(groups - 1 - len(ahead), lambda i: far_attend(i + len(ahead), far_weigh(i + len(ahead))))
     base = group * KV_HEADS
-    part_mine[pl.ds(base, KV_HEADS)] = out
-    for m in range(KV_HEADS):
-        first = m * block // 128 * 128
-        lse_mine[base + m] = lse[:, first:first + 128]
+    part_mine[pl.ds(base, KV_HEADS)] = attend(own_weighed)
     for target in mate_ids:
         send_out(target)
     part_all[me] = part_mine[me]
-    lse_all[me] = lse_mine[me]
 
     lse_wait = copy(lse_all.at[rest], lse_all.at[rest], l_send, l_recv, mate_ids[0])
-    out_wait = copy(part_all.at[rest], part_all.at[rest], o_send, o_recv, mate_ids[0])
     lse_wait.wait_recv()
     shares = [None] * blocks
     for m in range(KV_HEADS):
@@ -258,14 +273,36 @@
     for k in range(1, 128 // block):
         columns = jnp.where(place == k, turned[k * block:(k + 1) * block], columns)
 
-    out_wait.wait_recv()
+    def out_wait(which, count):
+        part_ref = part_all.at[pl.ds(0, count)]
+        return copy(part_ref, part_ref, o_send, o_recv.at[which], mate_ids[0])
+
+    width = per_group * HEAD_DIM
+
+    def add_group(which, done):
+        found = []
+        for m in range(KV_HEADS):
+            part_out = part_all[which * KV_HEADS + m].astype(jnp.float32)
+            found.append(done[m] + share_ref[which * KV_HEADS + m] * part_out)
+        return found
+
+    for source in range(blocks):
+        share_ref[source] = jnp.broadcast_to(columns[:, source:source + 1], (block, HEAD_DIM))
+    done = [jnp.zeros((block, HEAD_DIM), jnp.float32)] * KV_HEADS
+    out_wait(group, KV_HEADS - 1).wait_recv()
+    done = add_group(group, done)
+    if groups <= 4:
+        for i in range(groups - 1):
+            out_wait(source_at(i), KV_HEADS).wait_recv()
+            done = add_group(source_at(i), done)
+    else:
+        def more(i, done):
+            out_wait(source_at(i), KV_HEADS).wait_recv()
+            return tuple(add_group(source_at(i), list(done)))
+
+        done = lax.fori_loop(0, groups - 1, more, tuple(done))
     for m in range(KV_HEADS):
-        done = jnp.zeros((block, HEAD_DIM), jnp.float32)
-        for g in range(groups):
-            source = g * KV_HEADS + m
-            done = done + columns[:, source:source + 1] * part_all[source].astype(jnp.float32)
-        line = jnp.concatenate([done[h * rows:(h + 1) * rows] for h in range(per_group)], axis=1)
-        width = per_group * HEAD_DIM
+        line = jnp.concatenate([done[m][h * rows:(h + 1) * rows] for h in range(per_group)], axis=1)
         out_ref[:, m * width:(m + 1) * width] = line.astype(jnp.bfloat16)
 
     for c in q_copies + kv_copies:
@@ -280,7 +317,7 @@
     page_wait.wait_send()
     last_wait.wait_send()
     lse_wait.wait_send()
-    out_wait.wait_send()
+    copy(part_all.at[rest], part_all.at[rest], o_send, o_recv.at[0], mate_ids[0]).wait_send()
 
 
 def shards(queries, key_cache, value_cache, tile_page, row_last):
@@ -299,12 +336,13 @@
         out_specs=pl.BlockSpec(memory_space=pltpu.VMEM),
         scratch_shapes=[
             pltpu.VMEM((rows, width), bf16),
+            pltpu.VMEM(value_cache.shape, bf16),
             pltpu.SMEM((rows,), jnp.int32),
             pltpu.VMEM((KV_HEADS, block, HEAD_DIM), bf16),
             pltpu.VMEM((1, 128), jnp.int32),
             pltpu.VMEM((groups, KV_HEADS, block, HEAD_DIM), bf16),
             pltpu.VMEM((KV_HEADS, tokens, HEAD_DIM), bf16),
-            pltpu.VMEM((KV_HEADS, tokens, HEAD_DIM), bf16),
+            pltpu.VMEM((KV_HEADS, HEAD_DIM, tokens), bf16),
             pltpu.VMEM((KV_HEADS, HEAD_DIM, tokens), bf16),
             pltpu.VMEM((KV_HEADS, 1, tokens), jnp.int32),
             pltpu.VMEM((blocks, 1, 128), jnp.int32),
@@ -313,9 +351,10 @@
             pltpu.VMEM((blocks, block, HEAD_DIM), bf16),
             pltpu.VMEM((blocks, 1, 128), f32),
             pltpu.VMEM((blocks, 1, 128), f32),
+            pltpu.VMEM((blocks, block, HEAD_DIM), f32),
             dma((2,)), dma((3,)),
             quad, dma((blocks,)), dma((groups, 4)), quad, quad, quad, quad,
-            one, one, one, one, one, one, one, one,
+            one, one, one, one, one, dma((groups,)), one, one,
         ],
         compiler_params=pltpu.CompilerParams(
             collective_id=0, has_side_effects=True, vmem_limit_bytes=60 * 1024 * 1024

time: 24.7 us -> 25 us (1.012)
  Pallas kernels: 23 us -> 23.3 us
    pallas_call x1, Pallas kernels: 23 us -> 23.3 us  [shards(): pl.pallas_call(functools.partial(kernel, groups), out_shape=jax.ShapeDtyp...]
where the time goes in v3:
time: 25 us; the launch traced here: 24.8 us
  Pallas kernels  23.3 us (93%)
  local copies, waits for them, and re-layouts  1.47 us (6%)
    pallas_call x1, Pallas kernels, shards(): pl.pallas_call(functools.partial(kernel, groups), out_shape=jax.ShapeDtyp...  23.3 us
    unnamed x1, local copies, waits for them, and re-layouts  1.47 us

profile of v3, /device:TPU:0, one launch (start us, length us, event | category | flops | bytes accessed | tf_op | source)
XLA Modules:
  0.0 24.8 jit_solution(7435874034452426252)
XLA Ops:
  0.0 23.3 %shard_map.55 = bf16[8,4096]{1,0:T(8,128)(2,1)} custom-call(bf16[8,4096]{1,0:T(8,128)(2,1)} %q_hbm.1, bf16[256,512]{1,0:T(8,128)(2,1)} %k_hbm.1, bf16[256,512]{1,0:T(8,128)(2,1)} %v_hbm.1, s32[1,256]{1,0:T(1,128)} %bitcast.1, s32[8]{0:T(128)} %last_hbm.1), custom_call_target="tpu_custom_call" | custom-call | flops 540000000 | bytes 700000 | tf_op jit(solution)/shard_map/pallas_call | solution.py:332
  23.3 1.5 %copy.7 = bf16[8,4096]{1,0:T(8,128)(2,1)} copy(bf16[8,4096]{1,0:T(8,128)(2,1)} %shard_map.55) | data formatting | bytes 131072

commit v4 on v3

--- a/solution.py
+++ b/solution.py
@@ -44,16 +44,19 @@
     across = [lax.rem(member + 2, KV_HEADS), lax.rem(twin + 2, KV_HEADS)]
     mates = across + [twin]
     mate_ids = [group * KV_HEADS + m for m in mates]
-    order = sorted(range(1, groups), key=lambda s: -min(s, groups - s))
 
     def peer(i):
-        if groups <= 4:
-            return lax.rem(group + order[i], groups)
+        if groups == 4:
+            return (
+                lax.rem(group + 2, 4),
+                groups - 1 - group,
+                group + 1 - 2 * lax.rem(group, 2),
+            )[i]
         return lax.rem(group + 1 + i, groups)
 
     def source_at(i):
-        if groups <= 4:
-            return lax.rem(group + groups - order[i], groups)
+        if groups == 4:
+            return peer(i)
         return lax.rem(group + groups - 1 - i, groups)
 
     def copy(src, dst, send, recv, target):
@@ -102,11 +105,6 @@
 
     pl.semaphore_wait(barrier, blocks - 1)
 
-    q_copies = []
-    for i, (m, target) in enumerate(zip(mates, mate_ids)):
-        q_copies.append(copy(q_pack.at[m], q_all.at[group, member], q_send.at[i], q_recv.at[me], target))
-        q_copies[-1].start()
-
     def direct(i, k):
         m = (member, twin)[k]
         return copy(
@@ -125,13 +123,22 @@
         direct(i, 0).start()
         direct(i, 1).start()
 
+    q_copies, kv_copies = [], []
+
+    def send_q(i):
+        q_copies.append(copy(q_pack.at[mates[i]], q_all.at[group, member], q_send.at[i], q_recv.at[me], mate_ids[i]))
+        q_copies[-1].start()
+
+    def send_k(i):
+        columns = pl.ds(pl.multiple_of(mates[i] * HEAD_DIM, HEAD_DIM), HEAD_DIM)
+        kv_copies.append(copy(k_hbm.at[:, columns], k_all.at[member], k_send.at[i], k_recv.at[member], mate_ids[i]))
+        kv_copies[-1].start()
+
+    for send, i in ((send_q, 0), (send_q, 1), (send_k, 0), (send_k, 1)):
+        send(i)
     each(groups - 1, send_direct)
-
-    kv_copies = []
-    for i, (m, target) in enumerate(zip(mates, mate_ids)):
-        columns = pl.ds(pl.multiple_of(m * HEAD_DIM, HEAD_DIM), HEAD_DIM)
-        kv_copies.append(copy(k_hbm.at[:, columns], k_all.at[member], k_send.at[i], k_recv.at[member], target))
-        kv_copies[-1].start()
+    send_q(2)
+    send_k(2)
 
     def q_wait(index):
         g, m = lax.div(index, KV_HEADS), lax.rem(index, KV_HEADS)
@@ -357,7 +364,7 @@
             one, one, one, one, one, dma((groups,)), one, one,
         ],
         compiler_params=pltpu.CompilerParams(
-            collective_id=0, has_side_effects=True, vmem_limit_bytes=60 * 1024 * 1024
+            collective_id=0, has_side_effects=True, vmem_limit_bytes=55104 * 1024
         ),
         cost_estimate=pl.CostEstimate(flops=540_000_000, bytes_accessed=700_000, transcendentals=1_000_000),
     )(queries, key_cache, value_cache, tile_page.reshape(1, tokens), row_last)

time: 25 us -> 24.2 us (0.968)
  Pallas kernels: 23.3 us -> 22.7 us
    pallas_call x1, Pallas kernels: 23.3 us -> 22.7 us  [shards(): pl.pallas_call(functools.partial(kernel, groups), out_shape=jax.ShapeDtyp...]
    unnamed x1 -> x5, local copies, waits for them, and re-layouts: 1.47 us -> 1.33 us
where the time goes in v4:
time: 24.2 us; the launch traced here: 24 us
  Pallas kernels  22.7 us (94%)
  local copies, waits for them, and re-layouts  1.33 us (5%)
    pallas_call x1, Pallas kernels, shards(): pl.pallas_call(functools.partial(kernel, groups), out_shape=jax.ShapeDtyp...  22.7 us
    unnamed x5, local copies, waits for them, and re-layouts  1.33 us

profile of v4, /device:TPU:0, one launch (start us, length us, event | category | flops | bytes accessed | tf_op | source)
XLA Modules:
  0.0 24.0 jit_solution(5862020283460495125)
XLA Ops:
  0.0 0.0 copy-start.1
  0.0 0.0 copy-start
  0.0 0.7 %copy-done.1 = s32[8]{0:T(128)S(1)} copy-done((s32[8]{0:T(128)S(1)}, s32[8]{0:T(128)}, u32[]{:S(2)}) %copy-start.1) | copy-done | bytes 56
  0.7 0.0 copy-done
  0.7 22.7 %shard_map.55 = bf16[8,4096]{1,0:T(8,128)(2,1)S(1)} custom-call(bf16[8,4096]{1,0:T(8,128)(2,1)} %q_hbm.1, bf16[256,512]{1,0:T(8,128)(2,1)} %k_hbm.1, bf16[256,512]{1,0:T(8,128)(2,1)} %v_hbm.1, s32[1,256]{1,0:T(1,128)S(1)} %bitcast.1, s32[8]{0:T(128)S(1)} %copy-done.1), custom_call_target="tpu_custom_call" | custom-call | flops 540000000 | bytes 700000 | tf_op jit(solution)/shard_map/pallas_call | solution.py:339
  23.4 0.6 %copy.7 = bf16[8,4096]{1,0:T(8,128)(2,1)} copy(bf16[8,4096]{1,0:T(8,128)(2,1)S(1)} %shard_map.55) | data formatting | bytes 131072
Async XLA Ops:
  0.0 0.7 %copy-start.1 = (s32[8]{0:T(128)S(1)}, s32[8]{0:T(128)}, u32[]{:S(2)}) copy-start(s32[8]{0:T(128)} %last_hbm.1) | copy-start | bytes 100
  0.0 0.7 %copy-start = (s32[256]{0:T(256)S(1)}, s32[256]{0:T(256)}, u32[]{:S(2)}) copy-start(s32[256]{0:T(256)} %param.8) | copy-start | bytes 3076

commit v5 on v4

--- a/solution.py
+++ b/solution.py
@@ -13,7 +13,7 @@
 NEGATIVE_FILL = -1e30
 LOG2E = math.log2(math.e)
 MESH = pl.DeviceIdType.MESH
-AHEAD = 2
+AHEAD = 1
 
 
 def each(count, body):
@@ -144,6 +144,15 @@
         g, m = lax.div(index, KV_HEADS), lax.rem(index, KV_HEADS)
         copy(q_all.at[g, m], q_all.at[g, m], q_send.at[0], q_recv.at[index], mate_ids[0]).wait_recv()
 
+    q_wait(mate_ids[0])
+    q_wait(mate_ids[1])
+
+    def send_relay(i):
+        relay(i, 0).start()
+        relay(i, 1).start()
+
+    each(groups - 1, send_relay)
+
     load_v.wait()
     v_mine[...] = (
         v_in[...].astype(jnp.float32).T.astype(jnp.bfloat16).reshape(KV_HEADS, HEAD_DIM, tokens)
@@ -152,15 +161,6 @@
         kv_copies.append(copy(v_mine.at[m], v_all.at[member], v_send.at[i], v_recv.at[member], target))
         kv_copies[-1].start()
     v_all[member] = v_mine[member]
-
-    q_wait(mate_ids[0])
-    q_wait(mate_ids[1])
-
-    def send_relay(i):
-        relay(i, 0).start()
-        relay(i, 1).start()
-
-    each(groups - 1, send_relay)
 
     for target in mate_ids:
         copy(page_hbm, page_all.at[member], page_send, page_recv, target).start()

time: 24.2 us -> 24.2 us (level)
  no operation moved by 1% of the time
where the time goes in v5:
time: 24.2 us; the launch traced here: 23.9 us
  Pallas kernels  22.6 us (93%)
  local copies, waits for them, and re-layouts  1.33 us (5%)
    pallas_call x1, Pallas kernels, shards(): pl.pallas_call(functools.partial(kernel, groups), out_shape=jax.ShapeDtyp...  22.6 us
    unnamed x5, local copies, waits for them, and re-layouts  1.33 us

profile of v5, /device:TPU:0, one launch (start us, length us, event | category | flops | bytes accessed | tf_op | source)
XLA Modules:
  0.0 23.9 jit_solution(10696209840008027436)
XLA Ops:
  0.0 0.0 copy-start.1
  0.0 0.0 copy-start
  0.0 0.7 %copy-done.1 = s32[8]{0:T(128)S(1)} copy-done((s32[8]{0:T(128)S(1)}, s32[8]{0:T(128)}, u32[]{:S(2)}) %copy-start.1) | copy-done | bytes 56
  0.7 0.0 copy-done
  0.7 22.6 %shard_map.55 = bf16[8,4096]{1,0:T(8,128)(2,1)S(1)} custom-call(bf16[8,4096]{1,0:T(8,128)(2,1)} %q_hbm.1, bf16[256,512]{1,0:T(8,128)(2,1)} %k_hbm.1, bf16[256,512]{1,0:T(8,128)(2,1)} %v_hbm.1, s32[1,256]{1,0:T(1,128)S(1)} %bitcast.1, s32[8]{0:T(128)S(1)} %copy-done.1), custom_call_target="tpu_custom_call" | custom-call | flops 540000000 | bytes 700000 | tf_op jit(solution)/shard_map/pallas_call | solution.py:339
  23.3 0.6 %copy.7 = bf16[8,4096]{1,0:T(8,128)(2,1)} copy(bf16[8,4096]{1,0:T(8,128)(2,1)S(1)} %shard_map.55) | data formatting | bytes 131072
Async XLA Ops:
  0.0 0.7 %copy-start.1 = (s32[8]{0:T(128)S(1)}, s32[8]{0:T(128)}, u32[]{:S(2)}) copy-start(s32[8]{0:T(128)} %last_hbm.1) | copy-start | bytes 100
  0.0 0.7 %copy-start = (s32[256]{0:T(256)S(1)}, s32[256]{0:T(256)}, u32[]{:S(2)}) copy-start(s32[256]{0:T(256)} %param.8) | copy-start | bytes 3076
